TPU v7x, 256 devices: a whole 4x4x8 slice. The times are simulated.
256 devices in a mesh: tok: 32 (over x, y, core), head: 8 (over z).
Axes of the slice: x: 4, y: 4, z: 8, core: 2. Of those that a mesh axis runs over, the one named last changes fastest.
Arguments:
- queries: bfloat16 [8192, 8192], P(('tok', 'head')), may hold values from -5 to 5, as said below
- key_rows: bfloat16 [8192, 1024], P(('tok', 'head')), may hold values from -5 to 5, as said below
- value_rows: bfloat16 [8192, 1024], P(('tok', 'head')), may hold values from -5 to 5
- out_grad: bfloat16 [8192, 8192], P(('tok', 'head')), may hold values from -5 to 5
- lengths: int32 [8], replicated, may hold values from 1 to 2048, 8192 in all
- server_plan: int32 [1024], replicated, may hold values from 0 to 1023, as said below
Outputs:
- attended: bfloat16 [8192, 8192], P('tok', 'head')
- grad_query: bfloat16 [8192, 8192], P('tok', 'head')
- grad_key: bfloat16 [8192, 1024], P('tok', 'head')
- grad_value: bfloat16 [8192, 1024], P('tok', 'head')
- served_logsum: float32 [64, 8192], P('head', 'tok')
Inputs may be any that keep to these rules, and one draw needn't show every extreme that they name: `lengths`: the longest trajectory has exactly 2048 tokens. `server_plan`: a permutation of the 1024 query pieces (piece p holds tokens p * 8 to p * 8 + 7 and belongs to owner p // 32); server s holds entries s * 32 to s * 32 + 31; every server holds exactly one piece of every owner. `queries`: entries of order one. `key_rows`: entries of order one.
All inputs are finite; a program needn't handle non-finite values.
Results may differ from a plain program's by a relative error of at most 0.012.
Values may be sent and summed in bfloat16 or wider, within the bound.
A program may use at most 64 MiB of HBM per device.

v0:
```python
import jax
import jax.numpy as jnp
from jax import lax
from jax.sharding import PartitionSpec as P

HD = 128
WIN = 2048


masked_fill = -1e30


def segment_ids(lengths, count):
    ends = jnp.cumsum(lengths)
    position = jnp.arange(count, dtype=jnp.int32)
    return jnp.sum((ends[None, :] <= position[:, None]).astype(jnp.int32), axis=1)


def one_piece(query_block, grad_block, offset, gathered, trajectory, window_len):
    row_count = query_block.shape[0]
    kv_heads = gathered.shape[1] // (2 * HD)
    group_size = query_block.shape[1] // (kv_heads * HD)
    whole = gathered.shape[0]
    wstart = jnp.clip(offset + row_count - window_len, 0, whole - window_len).astype(jnp.int32)
    window = lax.dynamic_slice_in_dim(gathered, wstart, window_len, 0)
    key_block = window[:, : kv_heads * HD].reshape(window_len, kv_heads, HD)
    value_block = window[:, kv_heads * HD :].reshape(window_len, kv_heads, HD)
    query = query_block.reshape(row_count, kv_heads, group_size, HD)
    upstream = grad_block.reshape(row_count, kv_heads, group_size, HD)
    query_pos = offset + jnp.arange(row_count, dtype=jnp.int32)
    key_pos = wstart + jnp.arange(window_len, dtype=jnp.int32)
    query_seg = lax.dynamic_slice_in_dim(trajectory, offset, row_count, 0)
    key_seg = lax.dynamic_slice_in_dim(trajectory, wstart, window_len, 0)
    allowed = (query_seg[:, None] == key_seg[None, :]) & (key_pos[None, :] <= query_pos[:, None])
    inv_root = HD ** (-0.5)
    scores = (
        jnp.einsum("rkgd,mkd->kgrm", query, key_block, preferred_element_type=jnp.float32)
        * inv_root
    )
    scores = jnp.where(allowed[None, None], scores, masked_fill)
    row_max = jnp.max(scores, axis=-1, keepdims=True)
    raised = jnp.exp(scores - row_max)
    summed = jnp.sum(raised, axis=-1, keepdims=True)
    weights = raised / summed
    log_total = (row_max + jnp.log(summed))[..., 0]
    weights_low = lax.optimization_barrier(weights.astype(jnp.bfloat16))
    attended = jnp.einsum(
        "kgrm,mkd->rkgd", weights_low, value_block, preferred_element_type=jnp.float32
    )
    attended_low = lax.optimization_barrier(attended.astype(jnp.bfloat16))
    out_dot = jnp.sum(upstream.astype(jnp.float32) * attended_low.astype(jnp.float32), axis=-1)
    grad_weight = jnp.einsum(
        "rkgd,mkd->kgrm", upstream, value_block, preferred_element_type=jnp.float32
    )
    dscore = weights * (grad_weight - jnp.transpose(out_dot, (1, 2, 0))[..., None])
    dscore_low = lax.optimization_barrier(dscore.astype(jnp.bfloat16))
    dquery = (
        jnp.einsum("kgrm,mkd->rkgd", dscore_low, key_block, preferred_element_type=jnp.float32)
        * inv_root
    )
    grad_keys = (
        jnp.einsum("kgrm,rkgd->mkd", dscore_low, query, preferred_element_type=jnp.float32)
        * inv_root
    )
    grad_values = jnp.einsum(
        "kgrm,rkgd->mkd", weights_low, upstream, preferred_element_type=jnp.float32
    )
    window_grad = jnp.concatenate(
        [
            grad_keys.reshape(window_len, kv_heads * HD),
            grad_values.reshape(window_len, kv_heads * HD),
        ],
        axis=1,
    )
    return (
        attended_low.reshape(row_count, -1),
        dquery.astype(jnp.bfloat16).reshape(row_count, -1),
        log_total,
        wstart,
        window_grad,
    )


def serve_all(query_pieces, grad_pieces, offsets, gathered, trajectory, lengths, window_len):
    row_count = query_pieces.shape[1]
    spans = [window_len]
    while len(spans) < 5 and spans[-1] % 2 == 0 and (spans[-1] // 2 >= 2 * row_count):
        spans.append(spans[-1] // 2)
    span_table = jnp.array(spans, dtype=jnp.int32)
    starts = jnp.cumsum(lengths) - lengths
    traj_ids = jnp.arange(lengths.shape[0], dtype=jnp.int32)

    def make_branch(span):

        def run(operand):
            grad_total, query_block, grad_block, offset = operand
            attended, dquery, log_total, wstart, window_grad = one_piece(
                query_block, grad_block, offset, gathered, trajectory, span
            )
            previous = lax.dynamic_slice_in_dim(grad_total, wstart, span, 0)
            grad_total = lax.dynamic_update_slice_in_dim(
                grad_total, previous + window_grad, wstart, 0
            )
            return (grad_total, (attended, dquery, log_total))

        return run

    branches = [make_branch(span) for span in spans]

    def advance(grad_total, inputs):
        query_block, grad_block, offset = inputs
        piece_seg = lax.dynamic_slice_in_dim(trajectory, offset, 1, 0)[0]
        traj_start = jnp.sum(jnp.where(traj_ids == piece_seg, starts, 0))
        needed = offset + row_count - traj_start
        pick = jnp.sum((span_table >= needed).astype(jnp.int32)) - 1
        return lax.switch(pick, branches, (grad_total, query_block, grad_block, offset))

    initial = jnp.zeros((gathered.shape[0], gathered.shape[1]), jnp.float32)
    return lax.scan(advance, initial, (query_pieces, grad_pieces, offsets))


def body(queries, key_rows, value_rows, out_grad, lengths, server_plan):
    local_query, local_key, local_value, local_grad = (
        lax.all_to_all(queries, "head", split_axis=1, concat_axis=0, tiled=True),
        lax.all_to_all(key_rows, "head", split_axis=1, concat_axis=0, tiled=True),
        lax.all_to_all(value_rows, "head", split_axis=1, concat_axis=0, tiled=True),
        lax.all_to_all(out_grad, "head", split_axis=1, concat_axis=0, tiled=True),
    )
    tok_rows = local_query.shape[0]
    servers = lax.axis_size("tok")
    piece_rows = tok_rows // servers
    slot_count = tok_rows // piece_rows
    own_index = lax.axis_index("tok")
    gathered = lax.all_gather(
        jnp.concatenate([local_key, local_value], axis=1), "tok", axis=0, tiled=True
    )
    whole = gathered.shape[0]
    window_len = min(WIN, whole // 4)
    trajectory = segment_ids(lengths, whole)
    owned = own_index * slot_count + jnp.arange(slot_count, dtype=jnp.int32)
    flat_index = jnp.arange(server_plan.shape[0], dtype=jnp.int32)
    located = jnp.sum(
        jnp.where(server_plan[None, :] == owned[:, None], flat_index[None, :], 0), axis=1
    )
    target = located // slot_count
    served = lax.dynamic_slice_in_dim(server_plan, own_index * slot_count, slot_count, 0)
    source = served // slot_count
    server_ids = jnp.arange(servers, dtype=jnp.int32)
    query_pieces = local_query.reshape(slot_count, piece_rows, -1)
    grad_pieces = local_grad.reshape(slot_count, piece_rows, -1)
    select = (target[None, :] == server_ids[:, None]).astype(jnp.bfloat16)
    send_query = jnp.einsum(
        "si,ird->srd", select, query_pieces, preferred_element_type=jnp.float32
    ).astype(jnp.bfloat16)
    send_grad = jnp.einsum(
        "si,ird->srd", select, grad_pieces, preferred_element_type=jnp.float32
    ).astype(jnp.bfloat16)
    arrived_query, arrived_grad = (
        lax.all_to_all(send_query, "tok", split_axis=0, concat_axis=0, tiled=True),
        lax.all_to_all(send_grad, "tok", split_axis=0, concat_axis=0, tiled=True),
    )
    grad_total, (attended, dquery, log_total) = serve_all(
        jnp.take(arrived_query, source, axis=0),
        jnp.take(arrived_grad, source, axis=0),
        served * piece_rows,
        gathered,
        trajectory,
        lengths,
        window_len,
    )
    return_map = (source[None, :] == server_ids[:, None]).astype(jnp.bfloat16)
    back_out = jnp.einsum(
        "sj,jrd->srd",
        return_map,
        attended.reshape(slot_count, piece_rows, -1),
        preferred_element_type=jnp.float32,
    ).astype(jnp.bfloat16)
    back_grad = jnp.einsum(
        "sj,jrd->srd",
        return_map,
        dquery.reshape(slot_count, piece_rows, -1),
        preferred_element_type=jnp.float32,
    ).astype(jnp.bfloat16)
    arrived_out, arrived_dquery = (
        lax.all_to_all(back_out, "tok", split_axis=0, concat_axis=0, tiled=True),
        lax.all_to_all(back_grad, "tok", split_axis=0, concat_axis=0, tiled=True),
    )
    attended_rows = jnp.take(arrived_out, target, axis=0).reshape(tok_rows, -1)
    dquery_rows = jnp.take(arrived_dquery, target, axis=0).reshape(tok_rows, -1)
    grads = lax.psum_scatter(grad_total, "tok", scatter_dimension=0, tiled=True)
    kv_width = local_key.shape[1]
    grad_key = grads[:, :kv_width].astype(jnp.bfloat16)
    grad_value = grads[:, kv_width:].astype(jnp.bfloat16)
    log_rows = jnp.transpose(log_total.reshape(slot_count, -1, piece_rows), (1, 0, 2)).reshape(
        -1, tok_rows
    )
    return (attended_rows, dquery_rows, grad_key, grad_value, log_rows)


def solution(mesh):
    in_specs = (
        P(("tok", "head"), None),
        P(("tok", "head"), None),
        P(("tok", "head"), None),
        P(("tok", "head"), None),
        P(),
        P(),
    )
    out_specs = (
        P("tok", "head"),
        P("tok", "head"),
        P("tok", "head"),
        P("tok", "head"),
        P("head", "tok"),
    )
    return jax.shard_map(body, mesh=mesh, in_specs=in_specs, out_specs=out_specs, check_vma=False)
```

profile of v0, /device:TPU:1, one launch (start us, length us, event | category | flops | bytes accessed | tf_op | source)
XLA Modules:
  0.0 1123.4 jit_solution(7456259846628973213)
XLA Ops:
  8.7 9.0 all-to-all-start.4
  18.6 6.3 all-to-all-done.4
  24.9 9.6 all_to_all.90
  42.5 12.2 %all-to-all-done = bf16[32,8,1024]{2,0,1:T(8,128)(2,1)S(1)} async-done(((bf16[32,8,1024]{2,0,1:T(8,128)(2,1)}), bf16[32,8,1024]{2,0,1:T(8,128)(2,1)S(1)}, u32[]{:S(2)}, u32[]{:S(2)}) %all-to-all-start) | async-done | bytes 524320 | tf_op jit(solution)/shard_map/all_to_all | solution.py:124
  60.3 10.5 all-to-all-done.2
  70.8 12.8 %all-to-all-start.1 = ((bf16[32,8,1024]{2,1,0:T(8,128)(2,1)}), bf16[32,8,1024]{2,1,0:T(8,128)(2,1)S(1)}, u32[]{:S(2)}, u32[]{:S(2)}) async-start(bf16[32,8,1024]{2,1,0:T(8,128)(2,1)} %copy.312), calls=%async_computation.1 | async-start | bytes 1048576 | tf_op jit(solution)/shard_map/all_to_all | solution.py:159
  85.6 9.7 all-to-all-done.1
  100.2 10.3 all-to-all-done.3
  115.5 874.5 %while.20 = (s32[]{:T(128)}, f32[8192,256]{0,1:T(8,128)}, bf16[32,8,1024]{2,1,0:T(8,128)(2,1)}, bf16[32,8,1024]{2,1,0:T(8,128)(2,1)}, f32[32,1,8,8]{3,2,1,0:T(8,...) while((s32[]{:T(128)}, f32[8192,256]{0,1:T(8,128)}, ...), condition=%wide.region_26.28_spmd.clone.clone, body=%wide.region_3.27_spmd.sunk.clone.clone.sunk | while | flops 204449728 | bytes 18698976 | solution.py:119
  122.5 18.8 %conditional.5 = (f32[8192,256]{0,1:T(8,128)}, bf16[1,8,1024]{2,1,0:T(8,128)(2,1)}, bf16[1,8,1024]{2,1,0:T(8,128)(2,1)S(1)}, f32[1,1,8,8]{3,2,1,0:T(8,128)S(1)}) conditional(s32[]{:T(128)} %clamp.16, (s32[]{:T(128)}, f32[8192,256]{0,1:T(8,128)}, s32[8192]{0:T(1024)S(1)}, bf16[8192,256]{1,0:T(8,128)(2,1)}, ...), branch_computations={%region_6.10_spmd, %region_10.14_spmd, %region_14.18_spmd, %region... | conditional | flops 204449680 | bytes 18559298 | solution.py:116
  135.0 6.2 dynamic_update_slice.28
  150.2 25.5 %conditional.5 = (f32[8192,256]{0,1:T(8,128)}, bf16[1,8,1024]{2,1,0:T(8,128)(2,1)}, bf16[1,8,1024]{2,1,0:T(8,128)(2,1)S(1)}, f32[1,1,8,8]{3,2,1,0:T(8,128)S(1)}) conditional(s32[]{:T(128)} %clamp.16, (s32[]{:T(128)}, f32[8192,256]{0,1:T(8,128)}, s32[8192]{0:T(1024)S(1)}, bf16[8192,256]{1,0:T(8,128)(2,1)}, ...), branch_computations={%region_6.10_spmd, %region_10.14_spmd, %region_14.18_spmd, %region... | conditional | flops 204449680 | bytes 18559298 | solution.py:116
  164.4 11.3 %dynamic_update_slice.27 = f32[8192,256]{0,1:T(8,128)} dynamic-update-slice(f32[8192,256]{0,1:T(8,128)} %get-tuple-element.218, f32[2048,256]{0,1:T(8,128)S(1)} %maximum_add_fusion, s32[]{:T(128)S(6)} %min.11, s32[]{:T(128)} %constant.109.clone) | dynamic-update-slice | bytes 4194308 | tf_op jit(solution)/shard_map/while/body/eval_jaxpr/cond/branch_0_fun/dynamic_update_slice | solution.py:101
  184.6 15.5 %conditional.5 = (f32[8192,256]{0,1:T(8,128)}, bf16[1,8,1024]{2,1,0:T(8,128)(2,1)}, bf16[1,8,1024]{2,1,0:T(8,128)(2,1)S(1)}, f32[1,1,8,8]{3,2,1,0:T(8,128)S(1)}) conditional(s32[]{:T(128)} %clamp.16, (s32[]{:T(128)}, f32[8192,256]{0,1:T(8,128)}, s32[8192]{0:T(1024)S(1)}, bf16[8192,256]{1,0:T(8,128)(2,1)}, ...), branch_computations={%region_6.10_spmd, %region_10.14_spmd, %region_14.18_spmd, %region... | conditional | flops 204449680 | bytes 18559298 | solution.py:116
  209.0 13.4 %conditional.5 = (f32[8192,256]{0,1:T(8,128)}, bf16[1,8,1024]{2,1,0:T(8,128)(2,1)}, bf16[1,8,1024]{2,1,0:T(8,128)(2,1)S(1)}, f32[1,1,8,8]{3,2,1,0:T(8,128)S(1)}) conditional(s32[]{:T(128)} %clamp.16, (s32[]{:T(128)}, f32[8192,256]{0,1:T(8,128)}, s32[8192]{0:T(1024)S(1)}, bf16[8192,256]{1,0:T(8,128)(2,1)}, ...), branch_computations={%region_6.10_spmd, %region_10.14_spmd, %region_14.18_spmd, %region... | conditional | flops 204449680 | bytes 18559298 | solution.py:116
  231.3 18.8 %conditional.5 = (f32[8192,256]{0,1:T(8,128)}, bf16[1,8,1024]{2,1,0:T(8,128)(2,1)}, bf16[1,8,1024]{2,1,0:T(8,128)(2,1)S(1)}, f32[1,1,8,8]{3,2,1,0:T(8,128)S(1)}) conditional(s32[]{:T(128)} %clamp.16, (s32[]{:T(128)}, f32[8192,256]{0,1:T(8,128)}, s32[8192]{0:T(1024)S(1)}, bf16[8192,256]{1,0:T(8,128)(2,1)}, ...), branch_computations={%region_6.10_spmd, %region_10.14_spmd, %region_14.18_spmd, %region... | conditional | flops 204449680 | bytes 18559298 | solution.py:116
  243.9 6.2 dynamic_update_slice.28
  259.0 15.5 %conditional.5 = (f32[8192,256]{0,1:T(8,128)}, bf16[1,8,1024]{2,1,0:T(8,128)(2,1)}, bf16[1,8,1024]{2,1,0:T(8,128)(2,1)S(1)}, f32[1,1,8,8]{3,2,1,0:T(8,128)S(1)}) conditional(s32[]{:T(128)} %clamp.16, (s32[]{:T(128)}, f32[8192,256]{0,1:T(8,128)}, s32[8192]{0:T(1024)S(1)}, bf16[8192,256]{1,0:T(8,128)(2,1)}, ...), branch_computations={%region_6.10_spmd, %region_10.14_spmd, %region_14.18_spmd, %region... | conditional | flops 204449680 | bytes 18559298 | solution.py:116
  283.4 15.5 %conditional.5 = (f32[8192,256]{0,1:T(8,128)}, bf16[1,8,1024]{2,1,0:T(8,128)(2,1)}, bf16[1,8,1024]{2,1,0:T(8,128)(2,1)S(1)}, f32[1,1,8,8]{3,2,1,0:T(8,128)S(1)}) conditional(s32[]{:T(128)} %clamp.16, (s32[]{:T(128)}, f32[8192,256]{0,1:T(8,128)}, s32[8192]{0:T(1024)S(1)}, bf16[8192,256]{1,0:T(8,128)(2,1)}, ...), branch_computations={%region_6.10_spmd, %region_10.14_spmd, %region_14.18_spmd, %region... | conditional | flops 204449680 | bytes 18559298 | solution.py:116
  307.8 18.8 %conditional.5 = (f32[8192,256]{0,1:T(8,128)}, bf16[1,8,1024]{2,1,0:T(8,128)(2,1)}, bf16[1,8,1024]{2,1,0:T(8,128)(2,1)S(1)}, f32[1,1,8,8]{3,2,1,0:T(8,128)S(1)}) conditional(s32[]{:T(128)} %clamp.16, (s32[]{:T(128)}, f32[8192,256]{0,1:T(8,128)}, s32[8192]{0:T(1024)S(1)}, bf16[8192,256]{1,0:T(8,128)(2,1)}, ...), branch_computations={%region_6.10_spmd, %region_10.14_spmd, %region_14.18_spmd, %region... | conditional | flops 204449680 | bytes 18559298 | solution.py:116
  320.3 6.3 dynamic_update_slice.28
  335.5 12.6 %conditional.5 = (f32[8192,256]{0,1:T(8,128)}, bf16[1,8,1024]{2,1,0:T(8,128)(2,1)}, bf16[1,8,1024]{2,1,0:T(8,128)(2,1)S(1)}, f32[1,1,8,8]{3,2,1,0:T(8,128)S(1)}) conditional(s32[]{:T(128)} %clamp.16, (s32[]{:T(128)}, f32[8192,256]{0,1:T(8,128)}, s32[8192]{0:T(1024)S(1)}, bf16[8192,256]{1,0:T(8,128)(2,1)}, ...), branch_computations={%region_6.10_spmd, %region_10.14_spmd, %region_14.18_spmd, %region... | conditional | flops 204449680 | bytes 18559298 | solution.py:116
  357.1 18.8 %conditional.5 = (f32[8192,256]{0,1:T(8,128)}, bf16[1,8,1024]{2,1,0:T(8,128)(2,1)}, bf16[1,8,1024]{2,1,0:T(8,128)(2,1)S(1)}, f32[1,1,8,8]{3,2,1,0:T(8,128)S(1)}) conditional(s32[]{:T(128)} %clamp.16, (s32[]{:T(128)}, f32[8192,256]{0,1:T(8,128)}, s32[8192]{0:T(1024)S(1)}, bf16[8192,256]{1,0:T(8,128)(2,1)}, ...), branch_computations={%region_6.10_spmd, %region_10.14_spmd, %region_14.18_spmd, %region... | conditional | flops 204449680 | bytes 18559298 | solution.py:116
  369.6 6.3 dynamic_update_slice.28
  384.8 25.5 %conditional.5 = (f32[8192,256]{0,1:T(8,128)}, bf16[1,8,1024]{2,1,0:T(8,128)(2,1)}, bf16[1,8,1024]{2,1,0:T(8,128)(2,1)S(1)}, f32[1,1,8,8]{3,2,1,0:T(8,128)S(1)}) conditional(s32[]{:T(128)} %clamp.16, (s32[]{:T(128)}, f32[8192,256]{0,1:T(8,128)}, s32[8192]{0:T(1024)S(1)}, bf16[8192,256]{1,0:T(8,128)(2,1)}, ...), branch_computations={%region_6.10_spmd, %region_10.14_spmd, %region_14.18_spmd, %region... | conditional | flops 204449680 | bytes 18559298 | solution.py:116
  399.0 11.3 %dynamic_update_slice.27 = f32[8192,256]{0,1:T(8,128)} dynamic-update-slice(f32[8192,256]{0,1:T(8,128)} %get-tuple-element.218, f32[2048,256]{0,1:T(8,128)S(1)} %maximum_add_fusion, s32[]{:T(128)S(6)} %min.11, s32[]{:T(128)} %constant.109.clone) | dynamic-update-slice | bytes 4194308 | tf_op jit(solution)/shard_map/while/body/eval_jaxpr/cond/branch_0_fun/dynamic_update_slice | solution.py:101
  419.2 13.4 %conditional.5 = (f32[8192,256]{0,1:T(8,128)}, bf16[1,8,1024]{2,1,0:T(8,128)(2,1)}, bf16[1,8,1024]{2,1,0:T(8,128)(2,1)S(1)}, f32[1,1,8,8]{3,2,1,0:T(8,128)S(1)}) conditional(s32[]{:T(128)} %clamp.16, (s32[]{:T(128)}, f32[8192,256]{0,1:T(8,128)}, s32[8192]{0:T(1024)S(1)}, bf16[8192,256]{1,0:T(8,128)(2,1)}, ...), branch_computations={%region_6.10_spmd, %region_10.14_spmd, %region_14.18_spmd, %region... | conditional | flops 204449680 | bytes 18559298 | solution.py:116
  441.5 18.8 %conditional.5 = (f32[8192,256]{0,1:T(8,128)}, bf16[1,8,1024]{2,1,0:T(8,128)(2,1)}, bf16[1,8,1024]{2,1,0:T(8,128)(2,1)S(1)}, f32[1,1,8,8]{3,2,1,0:T(8,128)S(1)}) conditional(s32[]{:T(128)} %clamp.16, (s32[]{:T(128)}, f32[8192,256]{0,1:T(8,128)}, s32[8192]{0:T(1024)S(1)}, bf16[8192,256]{1,0:T(8,128)(2,1)}, ...), branch_computations={%region_6.10_spmd, %region_10.14_spmd, %region_14.18_spmd, %region... | conditional | flops 204449680 | bytes 18559298 | solution.py:116
  454.0 6.3 dynamic_update_slice.28
  469.2 15.5 %conditional.5 = (f32[8192,256]{0,1:T(8,128)}, bf16[1,8,1024]{2,1,0:T(8,128)(2,1)}, bf16[1,8,1024]{2,1,0:T(8,128)(2,1)S(1)}, f32[1,1,8,8]{3,2,1,0:T(8,128)S(1)}) conditional(s32[]{:T(128)} %clamp.16, (s32[]{:T(128)}, f32[8192,256]{0,1:T(8,128)}, s32[8192]{0:T(1024)S(1)}, bf16[8192,256]{1,0:T(8,128)(2,1)}, ...), branch_computations={%region_6.10_spmd, %region_10.14_spmd, %region_14.18_spmd, %region... | conditional | flops 204449680 | bytes 18559298 | solution.py:116
  493.7 18.8 %conditional.5 = (f32[8192,256]{0,1:T(8,128)}, bf16[1,8,1024]{2,1,0:T(8,128)(2,1)}, bf16[1,8,1024]{2,1,0:T(8,128)(2,1)S(1)}, f32[1,1,8,8]{3,2,1,0:T(8,128)S(1)}) conditional(s32[]{:T(128)} %clamp.16, (s32[]{:T(128)}, f32[8192,256]{0,1:T(8,128)}, s32[8192]{0:T(1024)S(1)}, bf16[8192,256]{1,0:T(8,128)(2,1)}, ...), branch_computations={%region_6.10_spmd, %region_10.14_spmd, %region_14.18_spmd, %region... | conditional | flops 204449680 | bytes 18559298 | solution.py:116
  506.2 6.2 dynamic_update_slice.28
  521.4 24.5 %conditional.5 = (f32[8192,256]{0,1:T(8,128)}, bf16[1,8,1024]{2,1,0:T(8,128)(2,1)}, bf16[1,8,1024]{2,1,0:T(8,128)(2,1)S(1)}, f32[1,1,8,8]{3,2,1,0:T(8,128)S(1)}) conditional(s32[]{:T(128)} %clamp.16, (s32[]{:T(128)}, f32[8192,256]{0,1:T(8,128)}, s32[8192]{0:T(1024)S(1)}, bf16[8192,256]{1,0:T(8,128)(2,1)}, ...), branch_computations={%region_6.10_spmd, %region_10.14_spmd, %region_14.18_spmd, %region... | conditional | flops 204449680 | bytes 18559298 | solution.py:116
  535.6 10.3 dynamic_update_slice.27
  554.8 15.5 %conditional.5 = (f32[8192,256]{0,1:T(8,128)}, bf16[1,8,1024]{2,1,0:T(8,128)(2,1)}, bf16[1,8,1024]{2,1,0:T(8,128)(2,1)S(1)}, f32[1,1,8,8]{3,2,1,0:T(8,128)S(1)}) conditional(s32[]{:T(128)} %clamp.16, (s32[]{:T(128)}, f32[8192,256]{0,1:T(8,128)}, s32[8192]{0:T(1024)S(1)}, bf16[8192,256]{1,0:T(8,128)(2,1)}, ...), branch_computations={%region_6.10_spmd, %region_10.14_spmd, %region_14.18_spmd, %region... | conditional | flops 204449680 | bytes 18559298 | solution.py:116
  579.2 25.1 %conditional.5 = (f32[8192,256]{0,1:T(8,128)}, bf16[1,8,1024]{2,1,0:T(8,128)(2,1)}, bf16[1,8,1024]{2,1,0:T(8,128)(2,1)S(1)}, f32[1,1,8,8]{3,2,1,0:T(8,128)S(1)}) conditional(s32[]{:T(128)} %clamp.16, (s32[]{:T(128)}, f32[8192,256]{0,1:T(8,128)}, s32[8192]{0:T(1024)S(1)}, bf16[8192,256]{1,0:T(8,128)(2,1)}, ...), branch_computations={%region_6.10_spmd, %region_10.14_spmd, %region_14.18_spmd, %region... | conditional | flops 204449680 | bytes 18559298 | solution.py:116
  593.4 10.9 dynamic_update_slice.27
  613.3 25.1 %conditional.5 = (f32[8192,256]{0,1:T(8,128)}, bf16[1,8,1024]{2,1,0:T(8,128)(2,1)}, bf16[1,8,1024]{2,1,0:T(8,128)(2,1)S(1)}, f32[1,1,8,8]{3,2,1,0:T(8,128)S(1)}) conditional(s32[]{:T(128)} %clamp.16, (s32[]{:T(128)}, f32[8192,256]{0,1:T(8,128)}, s32[8192]{0:T(1024)S(1)}, bf16[8192,256]{1,0:T(8,128)(2,1)}, ...), branch_computations={%region_6.10_spmd, %region_10.14_spmd, %region_14.18_spmd, %region... | conditional | flops 204449680 | bytes 18559298 | solution.py:116
  627.5 10.9 dynamic_update_slice.27
  647.3 13.2 %conditional.5 = (f32[8192,256]{0,1:T(8,128)}, bf16[1,8,1024]{2,1,0:T(8,128)(2,1)}, bf16[1,8,1024]{2,1,0:T(8,128)(2,1)S(1)}, f32[1,1,8,8]{3,2,1,0:T(8,128)S(1)}) conditional(s32[]{:T(128)} %clamp.16, (s32[]{:T(128)}, f32[8192,256]{0,1:T(8,128)}, s32[8192]{0:T(1024)S(1)}, bf16[8192,256]{1,0:T(8,128)(2,1)}, ...), branch_computations={%region_6.10_spmd, %region_10.14_spmd, %region_14.18_spmd, %region... | conditional | flops 204449680 | bytes 18559298 | solution.py:116
  669.3 12.4 %conditional.5 = (f32[8192,256]{0,1:T(8,128)}, bf16[1,8,1024]{2,1,0:T(8,128)(2,1)}, bf16[1,8,1024]{2,1,0:T(8,128)(2,1)S(1)}, f32[1,1,8,8]{3,2,1,0:T(8,128)S(1)}) conditional(s32[]{:T(128)} %clamp.16, (s32[]{:T(128)}, f32[8192,256]{0,1:T(8,128)}, s32[8192]{0:T(1024)S(1)}, bf16[8192,256]{1,0:T(8,128)(2,1)}, ...), branch_computations={%region_6.10_spmd, %region_10.14_spmd, %region_14.18_spmd, %region... | conditional | flops 204449680 | bytes 18559298 | solution.py:116
  690.7 18.8 %conditional.5 = (f32[8192,256]{0,1:T(8,128)}, bf16[1,8,1024]{2,1,0:T(8,128)(2,1)}, bf16[1,8,1024]{2,1,0:T(8,128)(2,1)S(1)}, f32[1,1,8,8]{3,2,1,0:T(8,128)S(1)}) conditional(s32[]{:T(128)} %clamp.16, (s32[]{:T(128)}, f32[8192,256]{0,1:T(8,128)}, s32[8192]{0:T(1024)S(1)}, bf16[8192,256]{1,0:T(8,128)(2,1)}, ...), branch_computations={%region_6.10_spmd, %region_10.14_spmd, %region_14.18_spmd, %region... | conditional | flops 204449680 | bytes 18559298 | solution.py:116
  703.2 6.2 dynamic_update_slice.28
  718.3 18.7 %conditional.5 = (f32[8192,256]{0,1:T(8,128)}, bf16[1,8,1024]{2,1,0:T(8,128)(2,1)}, bf16[1,8,1024]{2,1,0:T(8,128)(2,1)S(1)}, f32[1,1,8,8]{3,2,1,0:T(8,128)S(1)}) conditional(s32[]{:T(128)} %clamp.16, (s32[]{:T(128)}, f32[8192,256]{0,1:T(8,128)}, s32[8192]{0:T(1024)S(1)}, bf16[8192,256]{1,0:T(8,128)(2,1)}, ...), branch_computations={%region_6.10_spmd, %region_10.14_spmd, %region_14.18_spmd, %region... | conditional | flops 204449680 | bytes 18559298 | solution.py:116
  730.9 6.2 dynamic_update_slice.28
  746.0 18.8 %conditional.5 = (f32[8192,256]{0,1:T(8,128)}, bf16[1,8,1024]{2,1,0:T(8,128)(2,1)}, bf16[1,8,1024]{2,1,0:T(8,128)(2,1)S(1)}, f32[1,1,8,8]{3,2,1,0:T(8,128)S(1)}) conditional(s32[]{:T(128)} %clamp.16, (s32[]{:T(128)}, f32[8192,256]{0,1:T(8,128)}, s32[8192]{0:T(1024)S(1)}, bf16[8192,256]{1,0:T(8,128)(2,1)}, ...), branch_computations={%region_6.10_spmd, %region_10.14_spmd, %region_14.18_spmd, %region... | conditional | flops 204449680 | bytes 18559298 | solution.py:116
  758.5 6.3 dynamic_update_slice.28
  773.7 13.4 %conditional.5 = (f32[8192,256]{0,1:T(8,128)}, bf16[1,8,1024]{2,1,0:T(8,128)(2,1)}, bf16[1,8,1024]{2,1,0:T(8,128)(2,1)S(1)}, f32[1,1,8,8]{3,2,1,0:T(8,128)S(1)}) conditional(s32[]{:T(128)} %clamp.16, (s32[]{:T(128)}, f32[8192,256]{0,1:T(8,128)}, s32[8192]{0:T(1024)S(1)}, bf16[8192,256]{1,0:T(8,128)(2,1)}, ...), branch_computations={%region_6.10_spmd, %region_10.14_spmd, %region_14.18_spmd, %region... | conditional | flops 204449680 | bytes 18559298 | solution.py:116
  796.0 12.7 %conditional.5 = (f32[8192,256]{0,1:T(8,128)}, bf16[1,8,1024]{2,1,0:T(8,128)(2,1)}, bf16[1,8,1024]{2,1,0:T(8,128)(2,1)S(1)}, f32[1,1,8,8]{3,2,1,0:T(8,128)S(1)}) conditional(s32[]{:T(128)} %clamp.16, (s32[]{:T(128)}, f32[8192,256]{0,1:T(8,128)}, s32[8192]{0:T(1024)S(1)}, bf16[8192,256]{1,0:T(8,128)(2,1)}, ...), branch_computations={%region_6.10_spmd, %region_10.14_spmd, %region_14.18_spmd, %region... | conditional | flops 204449680 | bytes 18559298 | solution.py:116
  817.6 25.5 %conditional.5 = (f32[8192,256]{0,1:T(8,128)}, bf16[1,8,1024]{2,1,0:T(8,128)(2,1)}, bf16[1,8,1024]{2,1,0:T(8,128)(2,1)S(1)}, f32[1,1,8,8]{3,2,1,0:T(8,128)S(1)}) conditional(s32[]{:T(128)} %clamp.16, (s32[]{:T(128)}, f32[8192,256]{0,1:T(8,128)}, s32[8192]{0:T(1024)S(1)}, bf16[8192,256]{1,0:T(8,128)(2,1)}, ...), branch_computations={%region_6.10_spmd, %region_10.14_spmd, %region_14.18_spmd, %region... | conditional | flops 204449680 | bytes 18559298 | solution.py:116
  831.8 11.3 %dynamic_update_slice.27 = f32[8192,256]{0,1:T(8,128)} dynamic-update-slice(f32[8192,256]{0,1:T(8,128)} %get-tuple-element.218, f32[2048,256]{0,1:T(8,128)S(1)} %maximum_add_fusion, s32[]{:T(128)S(6)} %min.11, s32[]{:T(128)} %constant.109.clone) | dynamic-update-slice | bytes 4194308 | tf_op jit(solution)/shard_map/while/body/eval_jaxpr/cond/branch_0_fun/dynamic_update_slice | solution.py:101
  852.0 24.5 %conditional.5 = (f32[8192,256]{0,1:T(8,128)}, bf16[1,8,1024]{2,1,0:T(8,128)(2,1)}, bf16[1,8,1024]{2,1,0:T(8,128)(2,1)S(1)}, f32[1,1,8,8]{3,2,1,0:T(8,128)S(1)}) conditional(s32[]{:T(128)} %clamp.16, (s32[]{:T(128)}, f32[8192,256]{0,1:T(8,128)}, s32[8192]{0:T(1024)S(1)}, bf16[8192,256]{1,0:T(8,128)(2,1)}, ...), branch_computations={%region_6.10_spmd, %region_10.14_spmd, %region_14.18_spmd, %region... | conditional | flops 204449680 | bytes 18559298 | solution.py:116
  866.2 10.3 dynamic_update_slice.27
  885.4 25.5 %conditional.5 = (f32[8192,256]{0,1:T(8,128)}, bf16[1,8,1024]{2,1,0:T(8,128)(2,1)}, bf16[1,8,1024]{2,1,0:T(8,128)(2,1)S(1)}, f32[1,1,8,8]{3,2,1,0:T(8,128)S(1)}) conditional(s32[]{:T(128)} %clamp.16, (s32[]{:T(128)}, f32[8192,256]{0,1:T(8,128)}, s32[8192]{0:T(1024)S(1)}, bf16[8192,256]{1,0:T(8,128)(2,1)}, ...), branch_computations={%region_6.10_spmd, %region_10.14_spmd, %region_14.18_spmd, %region... | conditional | flops 204449680 | bytes 18559298 | solution.py:116
  899.6 11.3 %dynamic_update_slice.27 = f32[8192,256]{0,1:T(8,128)} dynamic-update-slice(f32[8192,256]{0,1:T(8,128)} %get-tuple-element.218, f32[2048,256]{0,1:T(8,128)S(1)} %maximum_add_fusion, s32[]{:T(128)S(6)} %min.11, s32[]{:T(128)} %constant.109.clone) | dynamic-update-slice | bytes 4194308 | tf_op jit(solution)/shard_map/while/body/eval_jaxpr/cond/branch_0_fun/dynamic_update_slice | solution.py:101
  919.8 18.8 %conditional.5 = (f32[8192,256]{0,1:T(8,128)}, bf16[1,8,1024]{2,1,0:T(8,128)(2,1)}, bf16[1,8,1024]{2,1,0:T(8,128)(2,1)S(1)}, f32[1,1,8,8]{3,2,1,0:T(8,128)S(1)}) conditional(s32[]{:T(128)} %clamp.16, (s32[]{:T(128)}, f32[8192,256]{0,1:T(8,128)}, s32[8192]{0:T(1024)S(1)}, bf16[8192,256]{1,0:T(8,128)(2,1)}, ...), branch_computations={%region_6.10_spmd, %region_10.14_spmd, %region_14.18_spmd, %region... | conditional | flops 204449680 | bytes 18559298 | solution.py:116
  932.3 6.3 dynamic_update_slice.28
  947.5 18.3 %conditional.5 = (f32[8192,256]{0,1:T(8,128)}, bf16[1,8,1024]{2,1,0:T(8,128)(2,1)}, bf16[1,8,1024]{2,1,0:T(8,128)(2,1)S(1)}, f32[1,1,8,8]{3,2,1,0:T(8,128)S(1)}) conditional(s32[]{:T(128)} %clamp.16, (s32[]{:T(128)}, f32[8192,256]{0,1:T(8,128)}, s32[8192]{0:T(1024)S(1)}, bf16[8192,256]{1,0:T(8,128)(2,1)}, ...), branch_computations={%region_6.10_spmd, %region_10.14_spmd, %region_14.18_spmd, %region... | conditional | flops 204449680 | bytes 18559298 | solution.py:116
  974.7 13.4 %conditional.5 = (f32[8192,256]{0,1:T(8,128)}, bf16[1,8,1024]{2,1,0:T(8,128)(2,1)}, bf16[1,8,1024]{2,1,0:T(8,128)(2,1)S(1)}, f32[1,1,8,8]{3,2,1,0:T(8,128)S(1)}) conditional(s32[]{:T(128)} %clamp.16, (s32[]{:T(128)}, f32[8192,256]{0,1:T(8,128)}, s32[8192]{0:T(1024)S(1)}, bf16[8192,256]{1,0:T(8,128)(2,1)}, ...), branch_computations={%region_6.10_spmd, %region_10.14_spmd, %region_14.18_spmd, %region... | conditional | flops 204449680 | bytes 18559298 | solution.py:116
  990.1 9.0 copy.322
  1002.0 27.3 %all-to-all-start.6 = ((bf16[32,8,1024]{2,1,0:T(8,128)(2,1)}), bf16[32,8,1024]{2,1,0:T(8,128)(2,1)S(1)}, u32[]{:S(2)}, u32[]{:S(2)}) async-start(bf16[32,8,1024]{2,1,0:T(8,128)(2,1)} %copy.319), calls=%async_computation.6 | async-start | bytes 1048576 | tf_op jit(solution)/shard_map/all_to_all | solution.py:185
  1031.2 9.8 all-to-all-done.6
  1046.0 10.2 all-to-all-done.7
  1058.0 56.9 %reduce-scatter.2.cloned.1.call-done = f32[256,256]{1,0:T(8,128)} async-done(((f32[8192,256]{1,0:T(8,128)}), f32[256,256]{1,0:T(8,128)}) %reduce-scatter.2.cloned.1.call-update) | async-done | bytes 262160 | tf_op jit(solution)/shard_map/reduce_scatter | solution.py:190
  (906 shorter events, 555.3 us)
Async XLA Ops:
  7.2 0.8 copy-start
  7.2 51.0 %copy-start.3 = (s32[1024]{0:T(1024)S(1)}, s32[1024]{0:T(1024)}, u32[]{:S(2)}) copy-start(s32[1024]{0:T(1024)} %param.21) | copy-start | bytes 12292
  8.7 16.3 %all-to-all-start.4 = ((bf16[32,8,128]{2,0,1:T(8,128)(2,1)}), bf16[32,8,128]{2,0,1:T(8,128)(2,1)S(1)}, u32[]{:S(2)}, u32[]{:S(2)}) async-start(bf16[32,8,128]{2,0,1:T(8,128)(2,1)} %copy_bitcast_fusion.3), calls=%async_computation.4 | async-start | bytes 131072 | tf_op jit(solution)/shard_map/all_to_all | solution.py:125
  17.7 93.6 %all-gather.2.cloned.1.call-start = ((), (), s32[]{:S(2)}) async-start(), calls=%async_computation.9 | async-start | bytes 4325376 | tf_op jit(solution)/shard_map/all_gather | solution.py:134
  37.1 17.6 %all-to-all-start = ((bf16[32,8,1024]{2,0,1:T(8,128)(2,1)}), bf16[32,8,1024]{2,0,1:T(8,128)(2,1)S(1)}, u32[]{:S(2)}, u32[]{:S(2)}) async-start(bf16[32,8,1024]{2,0,1:T(8,128)(2,1)} %bitcast.353), calls=%async_computation | async-start | bytes 1048576 | tf_op jit(solution)/shard_map/all_to_all | solution.py:124
  40.6 58.7 %copy-start.4 = (s32[8]{0:T(128)S(1)}, s32[8]{0:T(128)}, u32[]{:S(2)}) copy-start(s32[8]{0:T(128)} %param.20) | copy-start | bytes 100
  54.7 16.1 %all-to-all-start.2 = ((bf16[32,8,1024]{2,0,1:T(8,128)(2,1)}), bf16[32,8,1024]{2,0,1:T(8,128)(2,1)S(1)}, u32[]{:S(2)}, u32[]{:S(2)}) async-start(bf16[32,8,1024]{2,0,1:T(8,128)(2,1)} %bitcast.352), calls=%async_computation.2 | async-start | bytes 1048576 | tf_op jit(solution)/shard_map/all_to_all | solution.py:127
  70.8 24.5 %all-to-all-start.1 = ((bf16[32,8,1024]{2,1,0:T(8,128)(2,1)}), bf16[32,8,1024]{2,1,0:T(8,128)(2,1)S(1)}, u32[]{:S(2)}, u32[]{:S(2)}) async-start(bf16[32,8,1024]{2,1,0:T(8,128)(2,1)} %copy.312), calls=%async_computation.1 | async-start | bytes 1048576 | tf_op jit(solution)/shard_map/all_to_all | solution.py:159
  95.3 15.3 %all-to-all-start.3 = ((bf16[32,8,1024]{2,1,0:T(8,128)(2,1)}), bf16[32,8,1024]{2,1,0:T(8,128)(2,1)S(1)}, u32[]{:S(2)}, u32[]{:S(2)}) async-start(bf16[32,8,1024]{2,1,0:T(8,128)(2,1)} %copy.315), calls=%async_computation.3 | async-start | bytes 1048576 | tf_op jit(solution)/shard_map/all_to_all | solution.py:160
  99.0 1015.9 %reduce-scatter.2.cloned.1.call-start = ((), (), s32[]{:S(2)}) async-start(), calls=%async_computation.10 | async-start | bytes 8650752 | tf_op jit(solution)/shard_map/reduce_scatter | solution.py:190
  111.3 4.2 copy-start.5
  999.1 1.0 copy-start.2
  999.1 30.3 %copy-start.1 = (bf16[32,8,1024]{2,1,0:T(8,128)(2,1)S(1)}, bf16[32,8,1024]{2,1,0:T(8,128)(2,1)}, u32[]{:S(2)}) copy-start(bf16[32,8,1024]{2,1,0:T(8,128)(2,1)} %get-tuple-element.276) | copy-start | bytes 1572868
  1002.0 39.0 %all-to-all-start.6 = ((bf16[32,8,1024]{2,1,0:T(8,128)(2,1)}), bf16[32,8,1024]{2,1,0:T(8,128)(2,1)S(1)}, u32[]{:S(2)}, u32[]{:S(2)}) async-start(bf16[32,8,1024]{2,1,0:T(8,128)(2,1)} %copy.319), calls=%async_computation.6 | async-start | bytes 1048576 | tf_op jit(solution)/shard_map/all_to_all | solution.py:185
  1041.0 15.3 %all-to-all-start.7 = ((bf16[32,8,1024]{2,1,0:T(8,128)(2,1)}), bf16[32,8,1024]{2,1,0:T(8,128)(2,1)S(1)}, u32[]{:S(2)}, u32[]{:S(2)}) async-start(bf16[32,8,1024]{2,1,0:T(8,128)(2,1)} %copy.321), calls=%async_computation.7 | async-start | bytes 1048576 | tf_op jit(solution)/shard_map/all_to_all | solution.py:186
Sparse Core Ops, SparseCore 0:
  35.3 50.4 all-gather.1
  999.2 115.6 reduce-scatter.1
where the time goes:
time: 1140 us; the launch traced here: 1120 us
  local copies, waits for them, and re-layouts  328 us (29%)
  loops' own time  210 us (18%)
  matrix products  196 us (17%)
  other arithmetic  176 us (15%)
  waiting for transfers between devices  126 us (11%)
  starting transfers between devices  63.8 us (6%)
  between operations  14.3 us (1%)
    dynamic_update_slice x32, local copies, waits for them, and re-layouts, run(): lax.dynamic_update_slice_in_dim(grad_total, previous + window_grad, wstar...  191 us
    another operation x1, loops' own time, serve_all(): return lax.scan(advance, initial, (query_pieces, grad_pieces, offsets))  124 us
    another operation x32, loops' own time, advance(): lax.switch(pick, branches, (grad_total, query_block, grad_block, offset))  85.7 us
    dynamic_update_slice x96, local copies, waits for them, and re-layouts, serve_all(): return lax.scan(advance, initial, (query_pieces, grad_pieces, offsets))  61.8 us
    dot_general x32, matrix products, one_piece(): jnp.einsum('kgrm,mkd->rkgd', weights_low, value_block, preferred_element_...  59.4 us
    reduce_scatter x1, waiting for transfers between devices, body(): grads = lax.psum_scatter(grad_total, 'tok', scatter_dimension=0, tiled=True)  56.9 us
    add x32, other arithmetic, run(): previous + window_grad  51.1 us
    reduce_sum x32, other arithmetic, advance(): traj_start = jnp.sum(jnp.where(traj_ids == piece_seg, starts, 0))  41.1 us
  transfers between devices with their start and end apart: 9, of which 8 were waited for; matrix products, arithmetic and copies ran while one was open for 2% of the time, Pallas kernels for 0%

commit v1 on v0

v1 whole, which is shorter than its diff:
```python
import functools

import jax
import jax.numpy as jnp
from jax import lax
from jax.experimental import pallas as pl
from jax.experimental.pallas import tpu as pltpu
from jax.sharding import PartitionSpec as P

bf16, f32, i32 = jnp.bfloat16, jnp.float32, jnp.int32
HD = 128
T = 256
NW = 9
NT_ = 32
NH = 8
RB = T // NH
NCH = 4
NTRAJ = 8
SCALE = HD**-0.5
LOG2E = 1.4426950408889634
C = SCALE * LOG2E
BIG = 1e30
MESH = pl.DeviceIdType.MESH

NN, NT = ((1,), (0,)), ((1,), (1,))


def dot(a, b, dims):
    return lax.dot_general(a, b, (dims, ((), ())), preferred_element_type=f32)


def fwd_head(q, kv, maskq, maskk, s_scr, p_scr):
    qa = jnp.concatenate([q, maskq], axis=1)
    mx = None
    for w in range(NW):
        ka = jnp.concatenate([kv[w, :, :HD], maskk[w]], axis=1)
        s = dot(qa, ka, NT)
        if w == NW - 1:
            r = lax.broadcasted_iota(i32, (T, T), 0)
            c = lax.broadcasted_iota(i32, (T, T), 1)
            s = jnp.where(c <= r, s, -BIG)
        s_scr[:, w * T : (w + 1) * T] = s
        m2 = jnp.maximum(s[:, :HD], s[:, HD:])
        mx = m2 if mx is None else jnp.maximum(mx, m2)
    m = jnp.max(mx, axis=1, keepdims=True)
    acc = jnp.zeros((T, T), f32)
    ones = jnp.ones((T, HD), bf16)
    for w in range(NW):
        p = jnp.exp2((s_scr[:, w * T : (w + 1) * T] - m) * C).astype(bf16)
        p_scr[:, w * T : (w + 1) * T] = p
        va = jnp.concatenate([kv[w, :, HD:], ones], axis=1)
        acc = acc + dot(p, va, NN)
    l = acc[:, HD:]
    li = 1.0 / l
    att = (acc[:, :HD] * li).astype(bf16)
    return att, li, m * SCALE + jnp.log(l)


def bwd_head(q, do, kv, p_scr, att, li, dkv_t):
    dof = do.astype(f32)
    neg = -jnp.sum(dof * att.astype(f32), axis=1, keepdims=True)
    d1 = neg.astype(bf16).astype(f32)
    d2 = (neg - d1).astype(bf16).astype(f32)
    d3 = neg - d1 - d2
    lane = lax.broadcasted_iota(i32, (T, HD), 1)
    ext = jnp.where(
        lane == 0, d1, jnp.where(lane == 1, d2, jnp.where(lane == 2, d3, 0.0))
    ).astype(bf16)
    doa = jnp.concatenate([do, ext], axis=1)
    q_t = (q.astype(f32) * li * SCALE).astype(bf16).T
    do_t = (dof * li).astype(bf16).T
    ones = jnp.ones((T, HD), bf16)
    acc = jnp.zeros((T, HD), f32)
    for w in range(NW):
        p = p_scr[:, w * T : (w + 1) * T]
        va = jnp.concatenate([kv[w, :, HD:], ones], axis=1)
        ds = (p.astype(f32) * dot(doa, va, NT)).astype(bf16)
        acc = acc + dot(ds, kv[w, :, :HD], NN)
        dkv_t[w, :HD, :] += dot(q_t, ds, NN)
        dkv_t[w, HD:, :] += dot(do_t, p, NN)
    return (acc * li * SCALE).astype(bf16)


def kernel(
    q_in, k_in, v_in, do_in, lengths, plan,
    att_out, dq_out, dk_out, dv_out, ls_out,
    qbuf, dobuf, kv, maskq, maskk, s_scr, p_all, linv, lcol, lsend, lall, dkv_t, gsend, grecv,
    own_sem, z_send, kv_recv, q_recv, do_recv, w_send, w_recv, l_send, l_recv, g_send, g_recv,
):
    me_t, me_h = lax.axis_index("tok"), lax.axis_index("head")

    def tok_peer(d):
        return (lax.rem(me_t + d, NT_), me_h)

    def head_peer(d):
        return (me_t, lax.rem(me_h + d, NH))

    barrier = pltpu.get_barrier_semaphore()
    for d in range(1, NH):
        pl.semaphore_signal(barrier, inc=1, device_id=head_peer(d), device_id_type=MESH)

    @pl.loop(1, NT_)
    def _(d):
        pl.semaphore_signal(barrier, inc=1, device_id=tok_peer(d), device_id_type=MESH)

    pl.semaphore_wait(barrier, NH - 1 + NT_ - 1)

    rows = pl.ds(pl.multiple_of(me_h * RB, RB), RB)

    def remote(src, dst, send, recv, peer):
        return pltpu.make_async_remote_copy(
            src_ref=src, dst_ref=dst, send_sem=send, recv_sem=recv,
            device_id=peer, device_id_type=MESH,
        )

    def z_sends(d):
        h = lax.rem(me_h + d, NH)
        peer = (me_t, h)
        cols = pl.ds(pl.multiple_of(h * HD, HD), HD)
        remote(k_in.at[:, cols], kv.at[NW - 1, rows, :HD], z_send.at[0], kv_recv, peer).start()
        remote(v_in.at[:, cols], kv.at[NW - 1, rows, HD:], z_send.at[0], kv_recv, peer).start()

    def big_sends(src, buf, send, recv):
        for c in range(NCH):
            for d in range(1, NH):
                h = lax.rem(me_h + d, NH)
                cols = pl.ds(pl.multiple_of(h * NH * HD + c * T, T), T)
                remote(src.at[:, cols], buf.at[c, rows], send, recv.at[c], (me_t, h)).start()

    for d in range(1, NH):
        z_sends(d)
    big_sends(q_in, qbuf, z_send.at[1], q_recv)
    big_sends(do_in, dobuf, z_send.at[2], do_recv)

    own_cols = pl.ds(pl.multiple_of(me_h * HD, HD), HD)
    own = [
        (k_in.at[:, own_cols], kv.at[NW - 1, rows, :HD]),
        (v_in.at[:, own_cols], kv.at[NW - 1, rows, HD:]),
    ]
    for c in range(NCH):
        cols = pl.ds(pl.multiple_of(me_h * NH * HD + c * T, T), T)
        own.append((q_in.at[:, cols], qbuf.at[c, rows]))
        own.append((do_in.at[:, cols], dobuf.at[c, rows]))
    own = [pltpu.make_async_copy(s, t, own_sem.at[i]) for i, (s, t) in enumerate(own)]
    for copy in own:
        copy.start()

    lane = lax.broadcasted_iota(i32, (1, HD), 1)
    first = jnp.zeros((1, HD), i32)
    last = jnp.zeros((1, HD), i32)
    run = jnp.int32(0)
    for n in range(NTRAJ):
        first = jnp.where(lane == n, run, first)
        run = run + lengths[n]
        last = jnp.where(lane == n, run, last)
    row = lax.broadcasted_iota(i32, (T, HD), 0)
    for w in range(NW):
        pos = row + (me_t + w - (NW - 1)) * T
        inside = (pos >= first) & (pos < last)
        maskk[w] = jnp.where(inside, 0.0, 1.0).astype(bf16)
        if w == NW - 1:
            maskq[...] = jnp.where(inside, -BIG, 0.0).astype(bf16)
        dkv_t[w] = jnp.zeros((T, T), f32)
    lcol[...] = jnp.zeros((T, HD), f32)

    def all_bytes(ref, sem):
        pltpu.make_async_copy(ref, ref, sem).wait()

    for copy in own:
        copy.wait()
    all_bytes(kv.at[NW - 1, : T - RB], kv_recv)

    for d in range(1, NW):
        remote(kv.at[NW - 1], kv.at[NW - 1 - d], w_send, w_recv.at[d - 1], tok_peer(d)).start()
    for d in range(1, NW):
        all_bytes(kv.at[NW - 1 - d], w_recv.at[d - 1])

    @pl.loop(0, NCH)
    def _(c):
        all_bytes(qbuf.at[c, : T - RB], q_recv.at[c])
        for i in range(2):
            j = 2 * c + i
            att, li, ls = fwd_head(
                qbuf[c, :, i * HD : (i + 1) * HD], kv, maskq[...], maskk, s_scr, p_all.at[j]
            )
            linv[j] = li
            att_out[:, pl.ds(pl.multiple_of(j * HD, HD), HD)] = att
            lanes = lax.broadcasted_iota(i32, (T, HD), 1)
            lcol[...] = jnp.where(lanes == j, ls, lcol[...])

    flat = lcol[...].T[:NH]
    lsend[0] = flat[:, :HD]
    lsend[1] = flat[:, HD:]

    @pl.loop(1, NT_)
    def _(d):
        remote(lsend, lall.at[me_t], l_send, l_recv, tok_peer(d)).start()

    lall[me_t] = lsend[...]

    @pl.loop(0, NCH)
    def _(c):
        all_bytes(dobuf.at[c, : T - RB], do_recv.at[c])
        for i in range(2):
            j = 2 * c + i
            at = pl.ds(pl.multiple_of(j * HD, HD), HD)
            half = slice(i * HD, (i + 1) * HD)
            dq_out[:, at] = bwd_head(
                qbuf[c, :, half], dobuf[c, :, half], kv, p_all.at[j], att_out[:, at], linv[j], dkv_t
            )

    for w in range(NW - 1):
        gsend[w] = dkv_t[w].astype(bf16)
        remote(
            gsend.at[w], grecv.at[w], g_send, g_recv.at[w], tok_peer(NT_ - (NW - 1 - w))
        ).start()

    all_bytes(lall.at[: NT_ - 1], l_recv)
    lane = lax.broadcasted_iota(i32, (NH, HD), 1)
    for half in range(2):
        picked = jnp.zeros((NH, HD), f32)
        for n in range(16):
            piece = plan[me_t * 32 + half * 16 + n]
            owner, local = piece // 32, lax.rem(piece, 32)
            tile = lall[owner, local // 16]
            shift = lax.rem(8 * n - 8 * lax.rem(local, 16) + HD, HD)
            picked = jnp.where(lane // 8 == n, pltpu.roll(tile, shift, 1), picked)
        ls_out[:, half * HD : (half + 1) * HD] = picked

    total = dkv_t[NW - 1]
    for w in range(NW - 1):
        all_bytes(grecv.at[w], g_recv.at[w])
        total = total + grecv[w].astype(f32)
    dk_out[...] = total[:HD].T.astype(bf16)
    dv_out[...] = total[HD:].T.astype(bf16)

    all_bytes(kv.at[NW - 1, : T - RB], z_send.at[0])
    all_bytes(qbuf.at[:, : T - RB], z_send.at[1])
    all_bytes(dobuf.at[:, : T - RB], z_send.at[2])
    all_bytes(kv.at[: NW - 1], w_send)
    all_bytes(lall.at[: NT_ - 1], l_send)
    all_bytes(gsend, g_send)


def body(queries, key_rows, value_rows, out_grad, lengths, server_plan):
    any_spec = pl.BlockSpec(memory_space=pl.ANY)
    vmem = pl.BlockSpec(memory_space=pltpu.VMEM)
    smem = pl.BlockSpec(memory_space=pltpu.SMEM)
    dma, V = pltpu.SemaphoreType.DMA, pltpu.VMEM
    return pl.pallas_call(
        kernel,
        out_shape=[
            jax.ShapeDtypeStruct((T, NH * HD), bf16),
            jax.ShapeDtypeStruct((T, NH * HD), bf16),
            jax.ShapeDtypeStruct((T, HD), bf16),
            jax.ShapeDtypeStruct((T, HD), bf16),
            jax.ShapeDtypeStruct((NH, T), f32),
        ],
        in_specs=[any_spec] * 4 + [smem] * 2,
        out_specs=[vmem] * 5,
        scratch_shapes=[
            V((NCH, T, T), bf16),
            V((NCH, T, T), bf16),
            V((NW, T, 2 * HD), bf16),
            V((T, HD), bf16),
            V((NW, T, HD), bf16),
            V((T, NW * T), f32),
            V((NH, T, NW * T), bf16),
            V((NH, T, HD), f32),
            V((T, HD), f32),
            V((2, NH, HD), f32),
            V((NT_, 2, NH, HD), f32),
            V((NW, T, T), f32),
            V((NW - 1, T, T), bf16),
            V((NW - 1, T, T), bf16),
            dma((2 + 2 * NCH,)),
            dma((3,)),
            dma(()),
            dma((NCH,)),
            dma((NCH,)),
            dma(()),
            dma((NW - 1,)),
            dma(()),
            dma(()),
            dma(()),
            dma((NW - 1,)),
        ],
        compiler_params=pltpu.CompilerParams(
            collective_id=0, has_side_effects=True, vmem_limit_bytes=56 * 2**20
        ),
        cost_estimate=pl.CostEstimate(
            flops=8 * 10**9, bytes_accessed=6 * 2**20, transcendentals=5 * 10**6
        ),
        name="attention",
    )(queries, key_rows, value_rows, out_grad, lengths, server_plan)


def solution(mesh):
    in_specs = (
        P(("tok", "head"), None),
        P(("tok", "head"), None),
        P(("tok", "head"), None),
        P(("tok", "head"), None),
        P(),
        P(),
    )
    out_specs = (
        P("tok", "head"),
        P("tok", "head"),
        P("tok", "head"),
        P("tok", "head"),
        P("head", "tok"),
    )
    return jax.shard_map(body, mesh=mesh, in_specs=in_specs, out_specs=out_specs, check_vma=False)
```

time: 1140 us -> 95.2 us (0.08)
  the two profiles are of different devices: /device:TPU:1 before, /device:TPU:25 now
where the time goes in v1:
time: 95.2 us; the launch traced here: 94.9 us
  Pallas kernels  89.3 us (94%)
  local copies, waits for them, and re-layouts  4.95 us (5%)
    pallas_call x1, Pallas kernels, body(): pl.pallas_call(kernel, out_shape=[jax.ShapeDtypeStruct((T, NH * HD), bf16...  89.3 us
    unnamed x13, local copies, waits for them, and re-layouts  4.95 us

profile of v1, /device:TPU:25, one launch (start us, length us, event | category | flops | bytes accessed | tf_op | source)
XLA Modules:
  0.0 94.9 jit_solution(16697942663276627540)
XLA Ops:
  0.6 89.3 %attention.1 = (bf16[256,1024]{1,0:T(8,128)(2,1)}, bf16[256,1024]{1,0:T(8,128)(2,1)}, bf16[256,128]{1,0:T(8,128)(2,1)}, bf16[256,128]{1,0:T(8,128)(2,1)}, f32[8,256]{1,0:T(8,128)}) custom-call(bf16[32,8192]{1,0:T(8,128)(2,1)} %q_in.1, bf16[32,1024]{1,0:T(8,128)(2,1)} %k_in.1, bf16[32,1024]{1,0:T(8,128)(2,1)} %v_in.1, bf16[32,8192]{1,0:T(8,128)(2,1)} %do_in.1, ...), custom_call_target="tpu_custom_call" | custom-call | flops 8000000000 | bytes 6291456 | tf_op jit(solution)/shard_map/attention/pallas_call | solution.py:250
  90.0 0.0 copy-start
  90.0 1.9 %copy.16 = bf16[256,1024]{1,0:T(8,128)(2,1)} copy(bf16[256,1024]{1,0:T(8,128)(2,1)} %get-tuple-element.10) | data formatting | bytes 1048576
  91.9 0.0 copy-done
  91.9 0.0 copy-start.2
  91.9 0.8 copy.17
  92.7 0.1 copy-done.2
  92.8 0.0 copy-start.1
  92.8 0.6 copy.18
  93.4 0.2 copy-done.1
  93.6 0.0 copy-start.3
  93.6 0.6 copy.19
  94.3 0.1 copy-done.3
  94.3 0.6 copy.20
Async XLA Ops:
  90.0 1.9 %copy-start = (bf16[256,1024]{1,0:T(8,128)(2,1)S(1)}, bf16[256,1024]{1,0:T(8,128)(2,1)}, u32[]{:S(2)}) copy-start(bf16[256,1024]{1,0:T(8,128)(2,1)} %get-tuple-element.11) | copy-start | bytes 1572868
  91.9 0.9 copy-start.2
  92.8 0.9 copy-start.1
  93.6 0.7 copy-start.3

commit v2 on v1

v2 whole, which is shorter than its diff:
```python
import functools

import jax
import jax.numpy as jnp
from jax import lax
from jax.experimental import pallas as pl
from jax.experimental.pallas import tpu as pltpu
from jax.sharding import PartitionSpec as P

bf16, f32, i32 = jnp.bfloat16, jnp.float32, jnp.int32
HD = 128
T = 256
NW = 9
NT_ = 32
NH = 8
RB = T // NH
NCH = 4
GR = 4 * T
NY = 4
NTRAJ = 8
SCALE = HD**-0.5
LOG2E = 1.4426950408889634
C = SCALE * LOG2E
BIG = 1e30
MESH = pl.DeviceIdType.MESH

NN, NT = ((1,), (0,)), ((1,), (1,))


def dot(a, b, dims):
    return lax.dot_general(a, b, (dims, ((), ())), preferred_element_type=f32)


def rows_of(buf, c):
    return jnp.concatenate([buf[c, :, :HD], buf[c, :, HD:]], axis=0)


def group_of(buf, g):
    return jnp.concatenate([rows_of(buf, 2 * g), rows_of(buf, 2 * g + 1)], axis=0)


def scores(w, c, qbuf, kv, maskq, maskk, s_all, mx):
    q = rows_of(qbuf, c)
    mask = maskq[...]
    qa = jnp.concatenate([q, jnp.concatenate([mask, mask], axis=0)], axis=1)
    ka = jnp.concatenate([kv[w, 0], maskk[w]], axis=1)
    s = dot(qa, ka, NT)
    if w == NW - 1:
        r = lax.rem(lax.broadcasted_iota(i32, s.shape, 0), T)
        s = jnp.where(lax.broadcasted_iota(i32, s.shape, 1) <= r, s, -BIG)
    at = pl.ds(pl.multiple_of(c * 2 * T, 2 * T), 2 * T)
    s_all[at, w * T : (w + 1) * T] = s
    m = jnp.maximum(s[:, :HD], s[:, HD:])
    mx[at] = m if w == NW - 1 else jnp.maximum(mx[at], m)


def softmax(at, kv, s_all, mx, p_all):
    m = jnp.max(mx[at], axis=1, keepdims=True) * C
    acc = jnp.zeros((GR, 2 * HD), f32)
    ones = jnp.ones((T, HD), bf16)
    for w in range(NW):
        p = jnp.exp2(s_all[at, w * T : (w + 1) * T] * C - m).astype(bf16)
        p_all[at, w * T : (w + 1) * T] = p
        acc = acc + dot(p, jnp.concatenate([kv[w, 1], ones], axis=1), NN)
    l = acc[:, HD:]
    li = 1.0 / l
    return (acc[:, :HD] * li).astype(bf16), li, m * (1.0 / LOG2E) + jnp.log(l)


def with_out_dot(do, att):
    neg = -jnp.sum(do.astype(f32) * att.astype(f32), axis=1, keepdims=True)
    d1 = neg.astype(bf16).astype(f32)
    d2 = (neg - d1).astype(bf16).astype(f32)
    d3 = neg - d1 - d2
    lane = lax.broadcasted_iota(i32, do.shape, 1)
    ext = jnp.where(
        lane == 0, d1, jnp.where(lane == 1, d2, jnp.where(lane == 2, d3, 0.0))
    ).astype(bf16)
    return jnp.concatenate([do, ext], axis=1)


def kernel(
    q_in, k_in, v_in, do_in, lengths, plan,
    att_out, dq_out, dk_out, dv_out, ls_out,
    qbuf, dobuf, kv, maskq, maskk, s_all, mx, p_all, att, linv, lcol, lsend, lall, dkv_t,
    gs_out, gs_in, gy_out, gy_in, gx_out, gx_in,
    own_sem, z_send, kv_recv, q_recv, do_recv, w_send, wx_recv, wy_recv, ws_recv, l_send, l_recv,
    g_send, gs_recv, gy_recv, gx_recv,
):
    me_t, me_h = lax.axis_index("tok"), lax.axis_index("head")

    core = lax.rem(me_t, 2)
    y = lax.rem(me_t // 2, NY)
    x_up = (lax.rem(me_t + 2 * NY, NT_), me_h)
    x_down = (lax.rem(me_t + NT_ - 2 * NY, NT_), me_h)
    sibling = (me_t + 1 - 2 * core, me_h)

    def y_peer(d):
        return (me_t + 2 * (lax.rem(y + d, NY) - y), me_h)

    def tok_peer(d):
        return (lax.rem(me_t + d, NT_), me_h)

    def head_peer(d):
        return (me_t, lax.rem(me_h + d, NH))

    barrier = pltpu.get_barrier_semaphore()
    for d in range(1, NH):
        pl.semaphore_signal(barrier, inc=1, device_id=head_peer(d), device_id_type=MESH)

    @pl.loop(1, NT_)
    def _(d):
        pl.semaphore_signal(barrier, inc=1, device_id=tok_peer(d), device_id_type=MESH)

    pl.semaphore_wait(barrier, NH - 1 + NT_ - 1)

    rows = pl.ds(pl.multiple_of(me_h * RB, RB), RB)

    def remote(src, dst, send, recv, peer):
        return pltpu.make_async_remote_copy(
            src_ref=src, dst_ref=dst, send_sem=send, recv_sem=recv,
            device_id=peer, device_id_type=MESH,
        )

    def z_sends(d):
        h = lax.rem(me_h + d, NH)
        peer = (me_t, h)
        cols = pl.ds(pl.multiple_of(h * HD, HD), HD)
        remote(k_in.at[:, cols], kv.at[NW - 1, 0, rows], z_send.at[0], kv_recv, peer).start()
        remote(v_in.at[:, cols], kv.at[NW - 1, 1, rows], z_send.at[0], kv_recv, peer).start()

    def big_sends(src, buf, send, recv):
        for c in range(NCH):
            for d in range(1, NH):
                h = lax.rem(me_h + d, NH)
                cols = pl.ds(pl.multiple_of(h * NH * HD + c * T, T), T)
                remote(src.at[:, cols], buf.at[c, rows], send, recv.at[c], (me_t, h)).start()

    for d in range(1, NH):
        z_sends(d)
    big_sends(q_in, qbuf, z_send.at[1], q_recv)
    big_sends(do_in, dobuf, z_send.at[2], do_recv)

    own_cols = pl.ds(pl.multiple_of(me_h * HD, HD), HD)
    own = [
        (k_in.at[:, own_cols], kv.at[NW - 1, 0, rows]),
        (v_in.at[:, own_cols], kv.at[NW - 1, 1, rows]),
    ]
    for c in range(NCH):
        cols = pl.ds(pl.multiple_of(me_h * NH * HD + c * T, T), T)
        own.append((q_in.at[:, cols], qbuf.at[c, rows]))
        own.append((do_in.at[:, cols], dobuf.at[c, rows]))
    own = [pltpu.make_async_copy(s, t, own_sem.at[i]) for i, (s, t) in enumerate(own)]
    for copy in own:
        copy.start()

    lane = lax.broadcasted_iota(i32, (1, HD), 1)
    first = jnp.zeros((1, HD), i32)
    last = jnp.zeros((1, HD), i32)
    run = jnp.int32(0)
    for n in range(NTRAJ):
        first = jnp.where(lane == n, run, first)
        run = run + lengths[n]
        last = jnp.where(lane == n, run, last)
    row = lax.broadcasted_iota(i32, (T, HD), 0)
    for w in range(NW):
        pos = row + (me_t + w - (NW - 1)) * T
        inside = (pos >= first) & (pos < last)
        maskk[w] = jnp.where(inside, 0.0, 1.0).astype(bf16)
        if w == NW - 1:
            maskq[...] = jnp.where(inside, -BIG, 0.0).astype(bf16)
    lcol[...] = jnp.zeros((T, HD), f32)

    def all_bytes(ref, sem):
        pltpu.make_async_copy(ref, ref, sem).wait()

    for copy in own:
        copy.wait()
    all_bytes(kv.at[NW - 1, :, : T - RB], kv_recv)

    def window(src, dst, recv, peer):
        remote(kv.at[src], kv.at[dst], w_send, recv, peer).start()

    def share(d):
        i = d - core
        window(8 - 2 * d, 7 - 2 * i, ws_recv.at[i], sibling)

    window(8, 0, wx_recv, x_up)
    for d in (1, 3, 2):
        pl.when(y + d < NY)(lambda d=d: window(8, 8 - 2 * d, wy_recv.at[d - 1], y_peer(d)))
    pl.when(core == 0)(lambda: share(0))
    all_bytes(kv.at[0], wx_recv)
    for d in (1, 3, 2):
        pl.when(y + d >= NY)(lambda d=d: window(0, 8 - 2 * d, wy_recv.at[d - 1], y_peer(d)))
    pl.when(core == 1)(lambda: share(4))
    for d in (1, 3, 2):
        all_bytes(kv.at[8 - 2 * d], wy_recv.at[d - 1])
        share(d)

    for w in (8, 0, 6, 4, 2, 7, 5, 3, 1):
        if w % 2:
            all_bytes(kv.at[w], ws_recv.at[(7 - w) // 2])

        @pl.loop(0, NCH)
        def _(c):
            if w == NW - 1:
                all_bytes(qbuf.at[c, : T - RB], q_recv.at[c])
            scores(w, c, qbuf, kv, maskq, maskk, s_all, mx)

    @pl.loop(0, 2)
    def _(g):
        at = pl.ds(pl.multiple_of(g * GR, GR), GR)
        out, li, ls = softmax(at, kv, s_all, mx, p_all)
        att[at] = out
        linv[at] = li
        lanes = lax.broadcasted_iota(i32, (T, HD), 1)
        col = lcol[...]
        for i in range(4):
            col = jnp.where(lanes == 4 * g + i, ls[i * T : (i + 1) * T], col)
            att_out[:, pl.ds(pl.multiple_of((4 * g + i) * HD, HD), HD)] = out[i * T : (i + 1) * T]
        lcol[...] = col

    flat = lcol[...].T[:NH]
    lsend[0] = flat[:, :HD]
    lsend[1] = flat[:, HD:]

    @pl.loop(1, NT_)
    def _(d):
        remote(lsend, lall.at[me_t], l_send, l_recv, tok_peer(d)).start()

    lall[me_t] = lsend[...]

    def sib_send(p, i):
        gs_out[p, i] = dkv_t[p, 7 - 2 * i].astype(bf16)
        remote(gs_out.at[p, i], gs_in.at[p, i], g_send.at[0], gs_recv.at[p, i], sibling).start()

    def y_send(p, d):
        i = d - core
        all_bytes(gs_in.at[p, i], gs_recv.at[p, i])
        gy_out[p, d - 1] = (dkv_t[p, 8 - 2 * d] + gs_in[p, i].astype(f32)).astype(bf16)
        remote(
            gy_out.at[p, d - 1], gy_in.at[p, d - 1], g_send.at[1], gy_recv.at[p, d - 1], y_peer(NY - d)
        ).start()

    def only(cond, ref):
        return jnp.where(cond, ref.astype(f32), 0.0)

    def x_send(p):
        all_bytes(gs_in.at[p, 3 * core], gs_recv.at[p, 3 * core])
        total = dkv_t[p, 0] + only(core == 1, gs_in[p, 3 * core])
        for d in (1, 2, 3):
            all_bytes(gy_in.at[p, d - 1], gy_recv.at[p, d - 1])
            total = total + only(y + d >= NY, gy_in[p, d - 1])
        gx_out[p] = total.astype(bf16)
        remote(gx_out.at[p], gx_in.at[p], g_send.at[2], gx_recv.at[p], x_down).start()

    def summed(p):
        total = dkv_t[p, 8] + only(core == 0, gs_in[p, 3 * core])
        for d in (1, 2, 3):
            total = total + only(y + d < NY, gy_in[p, d - 1])
        all_bytes(gx_in.at[p], gx_recv.at[p])
        return (total + gx_in[p].astype(f32)).T.astype(bf16)

    def passed_on(p, w):
        if w % 2:
            sib_send(p, (7 - w) // 2)
        elif w not in (0, 8):
            y_send(p, (8 - w) // 2)

    order = (7, 5, 6, 3, 4, 1, 2, 0, 8)
    ones = jnp.ones((T, HD), bf16)
    for g in range(2):
        at = slice(g * GR, (g + 1) * GR)
        for c in (2 * g, 2 * g + 1):
            all_bytes(dobuf.at[c, : T - RB], do_recv.at[c])
        do = group_of(dobuf, g)
        li = linv[at]
        do_t = (do.astype(f32) * li).astype(bf16).T
        q_t = (group_of(qbuf, g).astype(f32) * li * SCALE).astype(bf16).T
        doa = with_out_dot(do, att[at])
        for w in order:
            dv = dot(do_t, p_all[at, w * T : (w + 1) * T], NN)
            if g == 0:
                dkv_t[1, w] = dv
            else:
                dkv_t[1, w] += dv
                passed_on(1, w)
        acc = jnp.zeros((GR, HD), f32)
        for w in order:
            p = p_all[at, w * T : (w + 1) * T]
            va = jnp.concatenate([kv[w, 1], ones], axis=1)
            ds = (p.astype(f32) * dot(doa, va, NT)).astype(bf16)
            acc = acc + dot(ds, kv[w, 0], NN)
            dk = dot(q_t, ds, NN)
            if g == 0:
                dkv_t[0, w] = dk
            else:
                dkv_t[0, w] += dk
                passed_on(0, w)
        dq = (acc * li * SCALE).astype(bf16)
        for i in range(4):
            dq_out[:, (4 * g + i) * HD : (4 * g + i + 1) * HD] = dq[i * T : (i + 1) * T]
    x_send(1)
    x_send(0)

    all_bytes(lall.at[: NT_ - 1], l_recv)
    lane = lax.broadcasted_iota(i32, (NH, HD), 1)
    for half in range(2):
        picked = jnp.zeros((NH, HD), f32)
        for n in range(16):
            piece = plan[me_t * 32 + half * 16 + n]
            owner, local = piece // 32, lax.rem(piece, 32)
            tile = lall[owner, local // 16]
            shift = lax.rem(8 * n - 8 * lax.rem(local, 16) + HD, HD)
            picked = jnp.where(lane // 8 == n, pltpu.roll(tile, shift, 1), picked)
        ls_out[:, half * HD : (half + 1) * HD] = picked

    dv_out[...] = summed(1)
    dk_out[...] = summed(0)

    all_bytes(kv.at[NW - 1, :, : T - RB], z_send.at[0])
    all_bytes(qbuf.at[:, : T - RB], z_send.at[1])
    all_bytes(dobuf.at[:, : T - RB], z_send.at[2])
    all_bytes(kv.at[: NW - 1], w_send)
    all_bytes(lall.at[: NT_ - 1], l_send)
    all_bytes(gs_out, g_send.at[0])
    all_bytes(gy_out, g_send.at[1])
    all_bytes(gx_out, g_send.at[2])


def body(queries, key_rows, value_rows, out_grad, lengths, server_plan):
    any_spec = pl.BlockSpec(memory_space=pl.ANY)
    vmem = pl.BlockSpec(memory_space=pltpu.VMEM)
    smem = pl.BlockSpec(memory_space=pltpu.SMEM)
    dma, V = pltpu.SemaphoreType.DMA, pltpu.VMEM
    return pl.pallas_call(
        kernel,
        out_shape=[
            jax.ShapeDtypeStruct((T, NH * HD), bf16),
            jax.ShapeDtypeStruct((T, NH * HD), bf16),
            jax.ShapeDtypeStruct((T, HD), bf16),
            jax.ShapeDtypeStruct((T, HD), bf16),
            jax.ShapeDtypeStruct((NH, T), f32),
        ],
        in_specs=[any_spec] * 4 + [smem] * 2,
        out_specs=[vmem] * 5,
        scratch_shapes=[
            V((NCH, T, T), bf16),
            V((NCH, T, T), bf16),
            V((NW, 2, T, HD), bf16),
            V((T, HD), bf16),
            V((NW, T, HD), bf16),
            V((NH * T, NW * T), f32),
            V((NH * T, HD), f32),
            V((NH * T, NW * T), bf16),
            V((NH * T, HD), bf16),
            V((NH * T, HD), f32),
            V((T, HD), f32),
            V((2, NH, HD), f32),
            V((NT_, 2, NH, HD), f32),
            V((2, NW, HD, T), f32),
            V((2, 4, HD, T), bf16),
            V((2, 4, HD, T), bf16),
            V((2, 3, HD, T), bf16),
            V((2, 3, HD, T), bf16),
            V((2, HD, T), bf16),
            V((2, HD, T), bf16),
            dma((2 + 2 * NCH,)),
            dma((3,)),
            dma(()),
            dma((NCH,)),
            dma((NCH,)),
            dma(()),
            dma(()),
            dma((3,)),
            dma((4,)),
            dma(()),
            dma(()),
            dma((3,)),
            dma((2, 4)),
            dma((2, 3)),
            dma((2,)),
        ],
        compiler_params=pltpu.CompilerParams(
            collective_id=0, has_side_effects=True, vmem_limit_bytes=56 * 2**20
        ),
        cost_estimate=pl.CostEstimate(
            flops=8 * 10**9, bytes_accessed=6 * 2**20, transcendentals=5 * 10**6
        ),
        name="attention",
    )(queries, key_rows, value_rows, out_grad, lengths, server_plan)


def solution(mesh):
    in_specs = (
        P(("tok", "head"), None),
        P(("tok", "head"), None),
        P(("tok", "head"), None),
        P(("tok", "head"), None),
        P(),
        P(),
    )
    out_specs = (
        P("tok", "head"),
        P("tok", "head"),
        P("tok", "head"),
        P("tok", "head"),
        P("head", "tok"),
    )
    return jax.shard_map(body, mesh=mesh, in_specs=in_specs, out_specs=out_specs, check_vma=False)
```

time: 95.2 us -> 69.7 us (0.73)
  the two profiles are of different devices: /device:TPU:25 before, /device:TPU:1 now
where the time goes in v2:
time: 69.7 us; the launch traced here: 69.4 us
  Pallas kernels  63.8 us (92%)
  local copies, waits for them, and re-layouts  4.95 us (7%)
    pallas_call x1, Pallas kernels, body(): pl.pallas_call(kernel, out_shape=[jax.ShapeDtypeStruct((T, NH * HD), bf16...  63.8 us
    unnamed x13, local copies, waits for them, and re-layouts  4.95 us

profile of v2, /device:TPU:1, one launch (start us, length us, event | category | flops | bytes accessed | tf_op | source)
XLA Modules:
  0.0 69.4 jit_solution(7904577361977323872)
XLA Ops:
  0.6 63.8 %attention.1 = (bf16[256,1024]{1,0:T(8,128)(2,1)}, bf16[256,1024]{1,0:T(8,128)(2,1)}, bf16[256,128]{1,0:T(8,128)(2,1)}, bf16[256,128]{1,0:T(8,128)(2,1)}, f32[8,256]{1,0:T(8,128)}) custom-call(bf16[32,8192]{1,0:T(8,128)(2,1)} %q_in.1, bf16[32,1024]{1,0:T(8,128)(2,1)} %k_in.1, bf16[32,1024]{1,0:T(8,128)(2,1)} %v_in.1, bf16[32,8192]{1,0:T(8,128)(2,1)} %do_in.1, ...), custom_call_target="tpu_custom_call" | custom-call | flops 8000000000 | bytes 6291456 | tf_op jit(solution)/shard_map/attention/pallas_call | solution.py:336
  64.4 0.0 copy-start
  64.4 1.9 %copy.16 = bf16[256,1024]{1,0:T(8,128)(2,1)} copy(bf16[256,1024]{1,0:T(8,128)(2,1)} %get-tuple-element.10) | data formatting | bytes 1048576
  66.4 0.0 copy-done
  66.4 0.0 copy-start.2
  66.4 0.8 %copy.17 = bf16[256,1024]{1,0:T(8,128)(2,1)} copy(bf16[256,1024]{1,0:T(8,128)(2,1)S(1)} %copy-done) | data formatting | bytes 1048576
  67.2 0.1 copy-done.2
  67.2 0.0 copy-start.1
  67.2 0.6 copy.18
  67.9 0.2 copy-done.1
  68.1 0.0 copy-start.3
  68.1 0.6 copy.19
  68.7 0.1 copy-done.3
  68.8 0.6 copy.20
Async XLA Ops:
  64.4 1.9 %copy-start = (bf16[256,1024]{1,0:T(8,128)(2,1)S(1)}, bf16[256,1024]{1,0:T(8,128)(2,1)}, u32[]{:S(2)}) copy-start(bf16[256,1024]{1,0:T(8,128)(2,1)} %get-tuple-element.11) | copy-start | bytes 1572868
  66.4 0.9 %copy-start.2 = (bf16[256,128]{1,0:T(8,128)(2,1)S(1)}, bf16[256,128]{1,0:T(8,128)(2,1)}, u32[]{:S(2)}) copy-start(bf16[256,128]{1,0:T(8,128)(2,1)} %get-tuple-element.12) | copy-start | bytes 196612
  67.2 0.9 %copy-start.1 = (bf16[256,128]{1,0:T(8,128)(2,1)S(1)}, bf16[256,128]{1,0:T(8,128)(2,1)}, u32[]{:S(2)}) copy-start(bf16[256,128]{1,0:T(8,128)(2,1)} %get-tuple-element.13) | copy-start | bytes 196612
  68.1 0.7 %copy-start.3 = (f32[8,256]{1,0:T(8,128)S(1)}, f32[8,256]{1,0:T(8,128)}, u32[]{:S(2)}) copy-start(f32[8,256]{1,0:T(8,128)} %get-tuple-element.14) | copy-start | bytes 24580

commit v3 on v2

--- a/solution.py
+++ b/solution.py
@@ -48,7 +48,7 @@
     if w == NW - 1:
         r = lax.rem(lax.broadcasted_iota(i32, s.shape, 0), T)
         s = jnp.where(lax.broadcasted_iota(i32, s.shape, 1) <= r, s, -BIG)
-    at = pl.ds(pl.multiple_of(c * 2 * T, 2 * T), 2 * T)
+    at = slice(c * 2 * T, (c + 1) * 2 * T)
     s_all[at, w * T : (w + 1) * T] = s
     m = jnp.maximum(s[:, :HD], s[:, HD:])
     mx[at] = m if w == NW - 1 else jnp.maximum(mx[at], m)
@@ -82,24 +82,25 @@
 def kernel(
     q_in, k_in, v_in, do_in, lengths, plan,
     att_out, dq_out, dk_out, dv_out, ls_out,
-    qbuf, dobuf, kv, maskq, maskk, s_all, mx, p_all, att, linv, lcol, lsend, lall, dkv_t,
-    gs_out, gs_in, gy_out, gy_in, gx_out, gx_in,
-    own_sem, z_send, kv_recv, q_recv, do_recv, w_send, wx_recv, wy_recv, ws_recv, l_send, l_recv,
-    g_send, gs_recv, gy_recv, gx_recv,
+    qbuf, dobuf, kv, maskq, maskk, s_all, mx, p_all, att, linv, lcol, lall, dkv_t,
+    gs_out, gs_in, gd_out, gd_in,
+    own_sem, z_send, kv_recv, q_recv, do_recv, w_send, wd_recv, ws_recv, l_send, l_recv,
+    g_send, gs_recv, gd_recv,
 ):
     me_t, me_h = lax.axis_index("tok"), lax.axis_index("head")
 
     core = lax.rem(me_t, 2)
     y = lax.rem(me_t // 2, NY)
-    x_up = (lax.rem(me_t + 2 * NY, NT_), me_h)
-    x_down = (lax.rem(me_t + NT_ - 2 * NY, NT_), me_h)
     sibling = (me_t + 1 - 2 * core, me_h)
 
     def y_peer(d):
         return (me_t + 2 * (lax.rem(y + d, NY) - y), me_h)
 
-    def tok_peer(d):
-        return (lax.rem(me_t + d, NT_), me_h)
+    def chip_peer(d):
+        return (lax.rem(me_t + NT_ + 2 * d, NT_), me_h)
+
+    def x_peer(d):
+        return (lax.rem(me_t + 2 * NY * d, NT_), me_h)
 
     def head_peer(d):
         return (me_t, lax.rem(me_h + d, NH))
@@ -108,11 +109,9 @@
     for d in range(1, NH):
         pl.semaphore_signal(barrier, inc=1, device_id=head_peer(d), device_id_type=MESH)
 
-    @pl.loop(1, NT_)
-    def _(d):
-        pl.semaphore_signal(barrier, inc=1, device_id=tok_peer(d), device_id_type=MESH)
-
-    pl.semaphore_wait(barrier, NH - 1 + NT_ - 1)
+    for peer in [sibling] + [chip_peer(d) for d in (1, 2, 3, 4, 8, -4, -3, -2, -1)]:
+        pl.semaphore_signal(barrier, inc=1, device_id=peer, device_id_type=MESH)
+    pl.semaphore_wait(barrier, NH - 1 + 10)
 
     rows = pl.ds(pl.multiple_of(me_h * RB, RB), RB)
 
@@ -129,17 +128,22 @@
         remote(k_in.at[:, cols], kv.at[NW - 1, 0, rows], z_send.at[0], kv_recv, peer).start()
         remote(v_in.at[:, cols], kv.at[NW - 1, 1, rows], z_send.at[0], kv_recv, peer).start()
 
-    def big_sends(src, buf, send, recv):
-        for c in range(NCH):
-            for d in range(1, NH):
-                h = lax.rem(me_h + d, NH)
-                cols = pl.ds(pl.multiple_of(h * NH * HD + c * T, T), T)
-                remote(src.at[:, cols], buf.at[c, rows], send, recv.at[c], (me_t, h)).start()
+    def big_send(c, src, buf, send, recv):
+        for d in range(1, NH):
+            h = lax.rem(me_h + d, NH)
+            cols = pl.ds(pl.multiple_of(h * NH * HD + c * T, T), T)
+            remote(src.at[:, cols], buf.at[c, rows], send, recv.at[c], (me_t, h)).start()
+
+    def q_send(c):
+        big_send(c, q_in, qbuf, z_send.at[1], q_recv)
+
+    def do_send(c):
+        big_send(c, do_in, dobuf, z_send.at[2], do_recv)
 
     for d in range(1, NH):
         z_sends(d)
-    big_sends(q_in, qbuf, z_send.at[1], q_recv)
-    big_sends(do_in, dobuf, z_send.at[2], do_recv)
+    q_send(0)
+    q_send(1)
 
     own_cols = pl.ds(pl.multiple_of(me_h * HD, HD), HD)
     own = [
@@ -185,26 +189,34 @@
         i = d - core
         window(8 - 2 * d, 7 - 2 * i, ws_recv.at[i], sibling)
 
-    window(8, 0, wx_recv, x_up)
-    for d in (1, 3, 2):
-        pl.when(y + d < NY)(lambda d=d: window(8, 8 - 2 * d, wy_recv.at[d - 1], y_peer(d)))
+    for d in range(1, 5):
+        window(8, 8 - 2 * d, wd_recv.at[d - 1], chip_peer(d))
     pl.when(core == 0)(lambda: share(0))
-    all_bytes(kv.at[0], wx_recv)
-    for d in (1, 3, 2):
-        pl.when(y + d >= NY)(lambda d=d: window(0, 8 - 2 * d, wy_recv.at[d - 1], y_peer(d)))
-    pl.when(core == 1)(lambda: share(4))
-    for d in (1, 3, 2):
-        all_bytes(kv.at[8 - 2 * d], wy_recv.at[d - 1])
-        share(d)
-
-    for w in (8, 0, 6, 4, 2, 7, 5, 3, 1):
+    q_send(2)
+    q_send(3)
+
+    def own_scores(c):
+        all_bytes(qbuf.at[c, : T - RB], q_recv.at[c])
+        scores(NW - 1, c, qbuf, kv, maskq, maskk, s_all, mx)
+
+    own_scores(0)
+    own_scores(1)
+    do_send(0)
+    do_send(1)
+    for d in range(1, 5):
+        all_bytes(kv.at[8 - 2 * d], wd_recv.at[d - 1])
+        if d < 3:
+            do_send(d + 1)
+        if d < 4:
+            share(d)
+        else:
+            pl.when(core == 1)(lambda: share(4))
+    own_scores(2)
+    own_scores(3)
+    for w in (0, 6, 4, 2, 7, 5, 3, 1):
         if w % 2:
             all_bytes(kv.at[w], ws_recv.at[(7 - w) // 2])
-
-        @pl.loop(0, NCH)
-        def _(c):
-            if w == NW - 1:
-                all_bytes(qbuf.at[c, : T - RB], q_recv.at[c])
+        for c in range(NCH):
             scores(w, c, qbuf, kv, maskq, maskk, s_all, mx)
 
     @pl.loop(0, 2)
@@ -221,70 +233,79 @@
         lcol[...] = col
 
     flat = lcol[...].T[:NH]
-    lsend[0] = flat[:, :HD]
-    lsend[1] = flat[:, HD:]
-
-    @pl.loop(1, NT_)
-    def _(d):
-        remote(lsend, lall.at[me_t], l_send, l_recv, tok_peer(d)).start()
-
-    lall[me_t] = lsend[...]
+    mine = core * 16 + y * 4 + me_t // 8
+    lall[mine, 0] = flat[:, :HD]
+    lall[mine, 1] = flat[:, HD:]
+
+    def l_share(index, count, recv, peer):
+        part = lall.at[pl.ds(index, count)]
+        remote(part, part, l_send, recv, peer).start()
+
+    for d in (1, 2, 3):
+        l_share(mine, 1, l_recv.at[d], x_peer(d))
+
+    def l_over_y():
+        for d in (1, 2, 3):
+            all_bytes(lall.at[:1], l_recv.at[d])
+        for d in (1, 2, 3):
+            l_share(core * 16 + y * 4, 4, l_recv.at[3 + d], y_peer(d))
+
+    def l_over_cores():
+        for d in (1, 2, 3):
+            all_bytes(lall.at[:4], l_recv.at[3 + d])
+        l_share(core * 16, 16, l_recv.at[0], sibling)
 
     def sib_send(p, i):
         gs_out[p, i] = dkv_t[p, 7 - 2 * i].astype(bf16)
         remote(gs_out.at[p, i], gs_in.at[p, i], g_send.at[0], gs_recv.at[p, i], sibling).start()
 
-    def y_send(p, d):
-        i = d - core
-        all_bytes(gs_in.at[p, i], gs_recv.at[p, i])
-        gy_out[p, d - 1] = (dkv_t[p, 8 - 2 * d] + gs_in[p, i].astype(f32)).astype(bf16)
-        remote(
-            gy_out.at[p, d - 1], gy_in.at[p, d - 1], g_send.at[1], gy_recv.at[p, d - 1], y_peer(NY - d)
-        ).start()
-
     def only(cond, ref):
         return jnp.where(cond, ref.astype(f32), 0.0)
 
-    def x_send(p):
-        all_bytes(gs_in.at[p, 3 * core], gs_recv.at[p, 3 * core])
-        total = dkv_t[p, 0] + only(core == 1, gs_in[p, 3 * core])
-        for d in (1, 2, 3):
-            all_bytes(gy_in.at[p, d - 1], gy_recv.at[p, d - 1])
-            total = total + only(y + d >= NY, gy_in[p, d - 1])
-        gx_out[p] = total.astype(bf16)
-        remote(gx_out.at[p], gx_in.at[p], g_send.at[2], gx_recv.at[p], x_down).start()
+    def from_sibling(p, i):
+        all_bytes(gs_in.at[p, i], gs_recv.at[p, i])
+        return gs_in[p, i]
+
+    def owner_send(p, d):
+        i = d - core if d < 4 else 3 * core
+        part = from_sibling(p, i)
+        part = part.astype(f32) if d < 4 else only(core == 1, part)
+        gd_out[p, d - 1] = (dkv_t[p, 8 - 2 * d] + part).astype(bf16)
+        remote(
+            gd_out.at[p, d - 1], gd_in.at[p, d - 1], g_send.at[1], gd_recv.at[p, d - 1], chip_peer(-d)
+        ).start()
 
     def summed(p):
         total = dkv_t[p, 8] + only(core == 0, gs_in[p, 3 * core])
-        for d in (1, 2, 3):
-            total = total + only(y + d < NY, gy_in[p, d - 1])
-        all_bytes(gx_in.at[p], gx_recv.at[p])
-        return (total + gx_in[p].astype(f32)).T.astype(bf16)
-
-    def passed_on(p, w):
-        if w % 2:
-            sib_send(p, (7 - w) // 2)
-        elif w not in (0, 8):
-            y_send(p, (8 - w) // 2)
-
-    order = (7, 5, 6, 3, 4, 1, 2, 0, 8)
+        for d in range(1, 5):
+            all_bytes(gd_in.at[p, d - 1], gd_recv.at[p, d - 1])
+            total = total + gd_in[p, d - 1].astype(f32)
+        return total.T.astype(bf16)
+
+    order = (7, 5, 3, 1, 6, 4, 2, 0, 8)
     ones = jnp.ones((T, HD), bf16)
     for g in range(2):
         at = slice(g * GR, (g + 1) * GR)
         for c in (2 * g, 2 * g + 1):
             all_bytes(dobuf.at[c, : T - RB], do_recv.at[c])
-        do = group_of(dobuf, g)
-        li = linv[at]
-        do_t = (do.astype(f32) * li).astype(bf16).T
-        q_t = (group_of(qbuf, g).astype(f32) * li * SCALE).astype(bf16).T
-        doa = with_out_dot(do, att[at])
+        do_t = (group_of(dobuf, g).astype(f32) * linv[at]).astype(bf16).T
         for w in order:
             dv = dot(do_t, p_all[at, w * T : (w + 1) * T], NN)
             if g == 0:
                 dkv_t[1, w] = dv
             else:
                 dkv_t[1, w] += dv
-                passed_on(1, w)
+                if w % 2:
+                    sib_send(1, (7 - w) // 2)
+    l_over_y()
+    for g in range(2):
+        at = slice(g * GR, (g + 1) * GR)
+        li = linv[at]
+        q_t = (group_of(qbuf, g).astype(f32) * li * SCALE).astype(bf16).T
+        doa = with_out_dot(group_of(dobuf, g), att[at])
+        if g == 0:
+            for d in range(1, 5):
+                owner_send(1, d)
         acc = jnp.zeros((GR, HD), f32)
         for w in order:
             p = p_all[at, w * T : (w + 1) * T]
@@ -296,20 +317,24 @@
                 dkv_t[0, w] = dk
             else:
                 dkv_t[0, w] += dk
-                passed_on(0, w)
+                if w % 2:
+                    sib_send(0, (7 - w) // 2)
+                elif w < 8:
+                    owner_send(0, (8 - w) // 2)
+        if g == 0:
+            l_over_cores()
         dq = (acc * li * SCALE).astype(bf16)
         for i in range(4):
             dq_out[:, (4 * g + i) * HD : (4 * g + i + 1) * HD] = dq[i * T : (i + 1) * T]
-    x_send(1)
-    x_send(0)
-
-    all_bytes(lall.at[: NT_ - 1], l_recv)
+
+    all_bytes(lall.at[:16], l_recv.at[0])
     lane = lax.broadcasted_iota(i32, (NH, HD), 1)
     for half in range(2):
         picked = jnp.zeros((NH, HD), f32)
         for n in range(16):
             piece = plan[me_t * 32 + half * 16 + n]
             owner, local = piece // 32, lax.rem(piece, 32)
+            owner = lax.rem(owner, 2) * 16 + lax.rem(owner // 2, 4) * 4 + owner // 8
             tile = lall[owner, local // 16]
             shift = lax.rem(8 * n - 8 * lax.rem(local, 16) + HD, HD)
             picked = jnp.where(lane // 8 == n, pltpu.roll(tile, shift, 1), picked)
@@ -322,10 +347,18 @@
     all_bytes(qbuf.at[:, : T - RB], z_send.at[1])
     all_bytes(dobuf.at[:, : T - RB], z_send.at[2])
     all_bytes(kv.at[: NW - 1], w_send)
-    all_bytes(lall.at[: NT_ - 1], l_send)
+    all_bytes(lall.at[: 3 + 12 + 16], l_send)
     all_bytes(gs_out, g_send.at[0])
-    all_bytes(gy_out, g_send.at[1])
-    all_bytes(gx_out, g_send.at[2])
+    all_bytes(gd_out, g_send.at[1])
+
+
+def hand_over(*refs):
+    sems = refs[-1]
+    copies = [pltpu.make_async_copy(refs[i], refs[5 + i], sems.at[i]) for i in range(5)]
+    for copy in copies:
+        copy.start()
+    for copy in copies:
+        copy.wait()
 
 
 def body(queries, key_rows, value_rows, out_grad, lengths, server_plan):
@@ -333,7 +366,7 @@
     vmem = pl.BlockSpec(memory_space=pltpu.VMEM)
     smem = pl.BlockSpec(memory_space=pltpu.SMEM)
     dma, V = pltpu.SemaphoreType.DMA, pltpu.VMEM
-    return pl.pallas_call(
+    outs = pl.pallas_call(
         kernel,
         out_shape=[
             jax.ShapeDtypeStruct((T, NH * HD), bf16),
@@ -356,30 +389,25 @@
             V((NH * T, HD), bf16),
             V((NH * T, HD), f32),
             V((T, HD), f32),
-            V((2, NH, HD), f32),
             V((NT_, 2, NH, HD), f32),
             V((2, NW, HD, T), f32),
             V((2, 4, HD, T), bf16),
             V((2, 4, HD, T), bf16),
-            V((2, 3, HD, T), bf16),
-            V((2, 3, HD, T), bf16),
-            V((2, HD, T), bf16),
-            V((2, HD, T), bf16),
+            V((2, 4, HD, T), bf16),
+            V((2, 4, HD, T), bf16),
             dma((2 + 2 * NCH,)),
             dma((3,)),
             dma(()),
             dma((NCH,)),
             dma((NCH,)),
             dma(()),
-            dma(()),
-            dma((3,)),
+            dma((4,)),
             dma((4,)),
             dma(()),
-            dma(()),
-            dma((3,)),
+            dma((7,)),
+            dma((2,)),
             dma((2, 4)),
-            dma((2, 3)),
-            dma((2,)),
+            dma((2, 4)),
         ],
         compiler_params=pltpu.CompilerParams(
             collective_id=0, has_side_effects=True, vmem_limit_bytes=56 * 2**20
@@ -389,6 +417,14 @@
         ),
         name="attention",
     )(queries, key_rows, value_rows, out_grad, lengths, server_plan)
+    return pl.pallas_call(
+        hand_over,
+        out_shape=[jax.ShapeDtypeStruct(a.shape, a.dtype) for a in outs],
+        in_specs=[vmem] * 5,
+        out_specs=[any_spec] * 5,
+        scratch_shapes=[dma((5,))],
+        name="hand_over",
+    )(*outs)
 
 
 def solution(mesh):

time: 69.7 us -> 60.8 us (0.87)
  local copies, waits for them, and re-layouts: 4.95 us -> 0 us
  Pallas kernels: 63.8 us -> 59.8 us
    pallas_call x1, Pallas kernels: 63.8 us -> 57.5 us  [body(): pl.pallas_call(kernel, out_shape=[jax.ShapeDtypeStruct((T, NH * HD), bf16...]
    unnamed x13 -> x0, local copies, waits for them, and re-layouts: 4.95 us -> none
    pallas_call x0 -> x1, Pallas kernels: none -> 2.27 us  [body(): pl.pallas_call(hand_over, out_shape=[jax.ShapeDtypeStruct(a.shape, a.dtyp...]
where the time goes in v3:
time: 60.8 us; the launch traced here: 60.6 us
  Pallas kernels  59.8 us (98%)
  between operations  0.8 us (1%)
    pallas_call x1, Pallas kernels, body(): pl.pallas_call(kernel, out_shape=[jax.ShapeDtypeStruct((T, NH * HD), bf16...  57.5 us
    pallas_call x1, Pallas kernels, body(): pl.pallas_call(hand_over, out_shape=[jax.ShapeDtypeStruct(a.shape, a.dtyp...  2.27 us

profile of v3, /device:TPU:1, one launch (start us, length us, event | category | flops | bytes accessed | tf_op | source)
XLA Modules:
  0.0 60.6 jit_solution(11359641970481122558)
XLA Ops:
  0.6 57.5 %attention.1 = (bf16[256,1024]{1,0:T(8,128)(2,1)}, bf16[256,1024]{1,0:T(8,128)(2,1)}, bf16[256,128]{1,0:T(8,128)(2,1)}, bf16[256,128]{1,0:T(8,128)(2,1)}, f32[8,256]{1,0:T(8,128)}) custom-call(bf16[32,8192]{1,0:T(8,128)(2,1)} %q_in.1, bf16[32,1024]{1,0:T(8,128)(2,1)} %k_in.1, bf16[32,1024]{1,0:T(8,128)(2,1)} %v_in.1, bf16[32,8192]{1,0:T(8,128)(2,1)} %do_in.1, ...), custom_call_target="tpu_custom_call" | custom-call | flops 8000000000 | bytes 6291456 | tf_op jit(solution)/shard_map/attention/pallas_call | solution.py:369
  58.2 2.3 %hand_over.1 = (bf16[256,1024]{1,0:T(8,128)(2,1)}, bf16[256,1024]{1,0:T(8,128)(2,1)}, bf16[256,128]{1,0:T(8,128)(2,1)}, bf16[256,128]{1,0:T(8,128)(2,1)}, f32[8,256]{1,0:T(8,128)}) custom-call(bf16[256,1024]{1,0:T(8,128)(2,1)} %get-tuple-element.10.refs_0_, bf16[256,1024]{1,0:T(8,128)(2,1)} %get-tuple-element.11.refs_1_, ...), custom_call_target="tpu_custom_call" | custom-call | tf_op jit(solution)/shard_map/hand_over/pallas_call | solution.py:420

commit v4 on v3

--- a/solution.py
+++ b/solution.py
@@ -259,30 +259,29 @@
         gs_out[p, i] = dkv_t[p, 7 - 2 * i].astype(bf16)
         remote(gs_out.at[p, i], gs_in.at[p, i], g_send.at[0], gs_recv.at[p, i], sibling).start()
 
-    def only(cond, ref):
-        return jnp.where(cond, ref.astype(f32), 0.0)
-
-    def from_sibling(p, i):
+    def add_sibling(p, w, i):
         all_bytes(gs_in.at[p, i], gs_recv.at[p, i])
-        return gs_in[p, i]
+        dkv_t[p, w] += gs_in[p, i].astype(f32)
 
     def owner_send(p, d):
-        i = d - core if d < 4 else 3 * core
-        part = from_sibling(p, i)
-        part = part.astype(f32) if d < 4 else only(core == 1, part)
-        gd_out[p, d - 1] = (dkv_t[p, 8 - 2 * d] + part).astype(bf16)
+        if d < 4:
+            add_sibling(p, 8 - 2 * d, d - core)
+        else:
+            pl.when(core == 1)(lambda: add_sibling(p, 0, 3))
+        gd_out[p, d - 1] = dkv_t[p, 8 - 2 * d].astype(bf16)
         remote(
             gd_out.at[p, d - 1], gd_in.at[p, d - 1], g_send.at[1], gd_recv.at[p, d - 1], chip_peer(-d)
         ).start()
 
     def summed(p):
-        total = dkv_t[p, 8] + only(core == 0, gs_in[p, 3 * core])
-        for d in range(1, 5):
+        pl.when(core == 0)(lambda: add_sibling(p, 8, 0))
+        total = dkv_t[p, 8]
+        for d in range(4, 0, -1):
             all_bytes(gd_in.at[p, d - 1], gd_recv.at[p, d - 1])
             total = total + gd_in[p, d - 1].astype(f32)
         return total.T.astype(bf16)
 
-    order = (7, 5, 3, 1, 6, 4, 2, 0, 8)
+    order = (1, 3, 5, 7, 0, 2, 4, 6, 8)
     ones = jnp.ones((T, HD), bf16)
     for g in range(2):
         at = slice(g * GR, (g + 1) * GR)
@@ -297,15 +296,11 @@
                 dkv_t[1, w] += dv
                 if w % 2:
                     sib_send(1, (7 - w) // 2)
-    l_over_y()
-    for g in range(2):
-        at = slice(g * GR, (g + 1) * GR)
+        if g == 0:
+            l_over_y()
         li = linv[at]
         q_t = (group_of(qbuf, g).astype(f32) * li * SCALE).astype(bf16).T
         doa = with_out_dot(group_of(dobuf, g), att[at])
-        if g == 0:
-            for d in range(1, 5):
-                owner_send(1, d)
         acc = jnp.zeros((GR, HD), f32)
         for w in order:
             p = p_all[at, w * T : (w + 1) * T]
@@ -321,6 +316,9 @@
                     sib_send(0, (7 - w) // 2)
                 elif w < 8:
                     owner_send(0, (8 - w) // 2)
+                if w == 5:
+                    for d in range(4, 0, -1):
+                        owner_send(1, d)
         if g == 0:
             l_over_cores()
         dq = (acc * li * SCALE).astype(bf16)
@@ -369,11 +367,11 @@
     outs = pl.pallas_call(
         kernel,
         out_shape=[
-            jax.ShapeDtypeStruct((T, NH * HD), bf16),
-            jax.ShapeDtypeStruct((T, NH * HD), bf16),
-            jax.ShapeDtypeStruct((T, HD), bf16),
-            jax.ShapeDtypeStruct((T, HD), bf16),
-            jax.ShapeDtypeStruct((NH, T), f32),
+            pltpu.VMEM((T, NH * HD), bf16),
+            pltpu.VMEM((T, NH * HD), bf16),
+            pltpu.VMEM((T, HD), bf16),
+            pltpu.VMEM((T, HD), bf16),
+            pltpu.VMEM((NH, T), f32),
         ],
         in_specs=[any_spec] * 4 + [smem] * 2,
         out_specs=[vmem] * 5,

time: 60.8 us -> 65.4 us (1.076)
  the two profiles are of different devices: /device:TPU:1 before, /device:TPU:26 now
where the time goes in v4:
time: 65.4 us; the launch traced here: 65.2 us
  Pallas kernels  60.9 us (93%)
  local copies, waits for them, and re-layouts  3.4 us (5%)
  between operations  0.83 us (1%)
    pallas_call x1, Pallas kernels, body(): pl.pallas_call(kernel, out_shape=[pltpu.VMEM((T, NH * HD), bf16), pltpu.V...  58.7 us
    unnamed x10, local copies, waits for them, and re-layouts  3.4 us
    pallas_call x1, Pallas kernels, body(): pl.pallas_call(hand_over, out_shape=[jax.ShapeDtypeStruct(a.shape, a.dtyp...  2.26 us

profile of v4, /device:TPU:26, one launch (start us, length us, event | category | flops | bytes accessed | tf_op | source)
XLA Modules:
  0.0 65.2 jit_solution(3650590021618438377)
XLA Ops:
  0.6 58.7 %attention.1 = (bf16[256,1024]{1,0:T(8,128)(2,1)S(1)}, bf16[256,1024]{1,0:T(8,128)(2,1)S(1)}, bf16[256,128]{1,0:T(8,128)(2,1)S(1)}, bf16[256,128]{1,0:T(8,128)(2,1)S(1)}, f32[8,256]{1,0:T(8,128)S(1)}) custom-call(bf16[32,8192]{1,0:T(8,128)(2,1)} %q_in.1, bf16[32,1024]{1,0:T(8,128)(2,1)} %k_in.1, bf16[32,1024]{1,0:T(8,128)(2,1)} %v_in.1, ...), custom_call_target="tpu_custom_call" | custom-call | flops 8000000000 | bytes 6291456 | tf_op jit(solution)/shard_map/attention/pallas_call | solution.py:367
  59.3 0.0 copy-start
  59.3 0.8 %copy-done = bf16[256,1024]{1,0:T(8,128)(2,1)} copy-done((bf16[256,1024]{1,0:T(8,128)(2,1)}, bf16[256,1024]{1,0:T(8,128)(2,1)S(1)}, u32[]{:S(2)}) %copy-start) | copy-done | bytes 524312
  60.1 0.0 copy-start.1
  60.1 0.8 %copy-done.1 = bf16[256,1024]{1,0:T(8,128)(2,1)} copy-done((bf16[256,1024]{1,0:T(8,128)(2,1)}, bf16[256,1024]{1,0:T(8,128)(2,1)S(1)}, u32[]{:S(2)}) %copy-start.1) | copy-done | bytes 524312
  60.9 0.0 copy-start.2
  60.9 0.6 copy-done.2
  61.5 0.0 copy-start.3
  61.5 0.6 copy-done.3
  62.1 0.0 copy-start.4
  62.1 0.6 copy-done.4
  62.7 2.3 %hand_over.1 = (bf16[256,1024]{1,0:T(8,128)(2,1)}, bf16[256,1024]{1,0:T(8,128)(2,1)}, bf16[256,128]{1,0:T(8,128)(2,1)}, bf16[256,128]{1,0:T(8,128)(2,1)}, f32[8,256]{1,0:T(8,128)}) custom-call(bf16[256,1024]{1,0:T(8,128)(2,1)} %copy-done, bf16[256,1024]{1,0:T(8,128)(2,1)} %copy-done.1, bf16[256,128]{1,0:T(8,128)(2,1)} %copy-done.2, ...), custom_call_target="tpu_custom_call" | custom-call | tf_op jit(solution)/shard_map/hand_over/pallas_call | solution.py:418
Async XLA Ops:
  59.3 0.8 %copy-start = (bf16[256,1024]{1,0:T(8,128)(2,1)}, bf16[256,1024]{1,0:T(8,128)(2,1)S(1)}, u32[]{:S(2)}) copy-start(bf16[256,1024]{1,0:T(8,128)(2,1)S(1)} %get-tuple-element.10.refs_0_) | copy-start | bytes 1572868
  60.1 0.8 %copy-start.1 = (bf16[256,1024]{1,0:T(8,128)(2,1)}, bf16[256,1024]{1,0:T(8,128)(2,1)S(1)}, u32[]{:S(2)}) copy-start(bf16[256,1024]{1,0:T(8,128)(2,1)S(1)} %get-tuple-element.11.refs_1_) | copy-start | bytes 1572868
  60.9 0.6 copy-start.2
  61.5 0.6 copy-start.3
  62.1 0.6 copy-start.4

commit v5 on v4

--- a/solution.py
+++ b/solution.py
@@ -121,12 +121,12 @@
             device_id=peer, device_id_type=MESH,
         )
 
-    def z_sends(d):
-        h = lax.rem(me_h + d, NH)
-        peer = (me_t, h)
-        cols = pl.ds(pl.multiple_of(h * HD, HD), HD)
-        remote(k_in.at[:, cols], kv.at[NW - 1, 0, rows], z_send.at[0], kv_recv, peer).start()
-        remote(v_in.at[:, cols], kv.at[NW - 1, 1, rows], z_send.at[0], kv_recv, peer).start()
+    def kv_send(part, src):
+        for d in range(1, NH):
+            h = lax.rem(me_h + d, NH)
+            cols = pl.ds(pl.multiple_of(h * HD, HD), HD)
+            dst = kv.at[NW - 1, part, rows]
+            remote(src.at[:, cols], dst, z_send.at[0], kv_recv.at[part], (me_t, h)).start()
 
     def big_send(c, src, buf, send, recv):
         for d in range(1, NH):
@@ -140,10 +140,8 @@
     def do_send(c):
         big_send(c, do_in, dobuf, z_send.at[2], do_recv)
 
-    for d in range(1, NH):
-        z_sends(d)
-    q_send(0)
-    q_send(1)
+    kv_send(0, k_in)
+    kv_send(1, v_in)
 
     own_cols = pl.ds(pl.multiple_of(me_h * HD, HD), HD)
     own = [
@@ -174,63 +172,78 @@
         if w == NW - 1:
             maskq[...] = jnp.where(inside, -BIG, 0.0).astype(bf16)
     lcol[...] = jnp.zeros((T, HD), f32)
+    q_send(0)
+    q_send(1)
 
     def all_bytes(ref, sem):
         pltpu.make_async_copy(ref, ref, sem).wait()
 
     for copy in own:
         copy.wait()
-    all_bytes(kv.at[NW - 1, :, : T - RB], kv_recv)
-
-    def window(src, dst, recv, peer):
-        remote(kv.at[src], kv.at[dst], w_send, recv, peer).start()
-
-    def share(d):
+    def window(part, src, dst, recv, peer):
+        remote(kv.at[src, part], kv.at[dst, part], w_send, recv, peer).start()
+
+    def share(part, d):
         i = d - core
-        window(8 - 2 * d, 7 - 2 * i, ws_recv.at[i], sibling)
-
-    for d in range(1, 5):
-        window(8, 8 - 2 * d, wd_recv.at[d - 1], chip_peer(d))
-    pl.when(core == 0)(lambda: share(0))
-    q_send(2)
-    q_send(3)
+        window(part, 8 - 2 * d, 7 - 2 * i, ws_recv.at[part, i], sibling)
+
+    def spread(part):
+        all_bytes(kv.at[NW - 1, part, : T - RB], kv_recv.at[part])
+        for d in range(1, 5):
+            window(part, 8, 8 - 2 * d, wd_recv.at[part, d - 1], chip_peer(d))
+        pl.when(core == 0)(lambda: share(part, 0))
+
+    def pass_across(part):
+        for d in range(1, 5):
+            all_bytes(kv.at[8 - 2 * d, part], wd_recv.at[part, d - 1])
+            if d < 4:
+                share(part, d)
+            else:
+                pl.when(core == 1)(lambda: share(part, 4))
 
     def own_scores(c):
         all_bytes(qbuf.at[c, : T - RB], q_recv.at[c])
         scores(NW - 1, c, qbuf, kv, maskq, maskk, s_all, mx)
 
-    own_scores(0)
-    own_scores(1)
-    do_send(0)
-    do_send(1)
-    for d in range(1, 5):
-        all_bytes(kv.at[8 - 2 * d], wd_recv.at[d - 1])
-        if d < 3:
-            do_send(d + 1)
-        if d < 4:
-            share(d)
-        else:
-            pl.when(core == 1)(lambda: share(4))
-    own_scores(2)
-    own_scores(3)
-    for w in (0, 6, 4, 2, 7, 5, 3, 1):
-        if w % 2:
-            all_bytes(kv.at[w], ws_recv.at[(7 - w) // 2])
-        for c in range(NCH):
-            scores(w, c, qbuf, kv, maskq, maskk, s_all, mx)
-
-    @pl.loop(0, 2)
-    def _(g):
-        at = pl.ds(pl.multiple_of(g * GR, GR), GR)
+    def soft(g):
+        at = slice(g * GR, (g + 1) * GR)
         out, li, ls = softmax(at, kv, s_all, mx, p_all)
         att[at] = out
         linv[at] = li
         lanes = lax.broadcasted_iota(i32, (T, HD), 1)
         col = lcol[...]
         for i in range(4):
-            col = jnp.where(lanes == 4 * g + i, ls[i * T : (i + 1) * T], col)
-            att_out[:, pl.ds(pl.multiple_of((4 * g + i) * HD, HD), HD)] = out[i * T : (i + 1) * T]
+            j = 4 * g + i
+            col = jnp.where(lanes == j, ls[i * T : (i + 1) * T], col)
+            att_out[:, j * HD : (j + 1) * HD] = out[i * T : (i + 1) * T]
         lcol[...] = col
+
+    spread(0)
+    q_send(2)
+    spread(1)
+    q_send(3)
+    own_scores(0)
+    pass_across(0)
+    do_send(0)
+    own_scores(1)
+    for w in (6, 4, 2, 0, 7, 5, 3, 1):
+        if w % 2:
+            all_bytes(kv.at[w, 0], ws_recv.at[0, (7 - w) // 2])
+        for c in (0, 1):
+            scores(w, c, qbuf, kv, maskq, maskk, s_all, mx)
+    do_send(1)
+    pass_across(1)
+    do_send(2)
+    for i in range(4):
+        all_bytes(kv.at[7 - 2 * i, 1], ws_recv.at[1, i])
+    soft(0)
+    do_send(3)
+    own_scores(2)
+    own_scores(3)
+    for w in (6, 4, 2, 0, 7, 5, 3, 1):
+        for c in (2, 3):
+            scores(w, c, qbuf, kv, maskq, maskk, s_all, mx)
+    soft(1)
 
     flat = lcol[...].T[:NH]
     mine = core * 16 + y * 4 + me_t // 8
@@ -367,11 +380,11 @@
     outs = pl.pallas_call(
         kernel,
         out_shape=[
-            pltpu.VMEM((T, NH * HD), bf16),
-            pltpu.VMEM((T, NH * HD), bf16),
-            pltpu.VMEM((T, HD), bf16),
-            pltpu.VMEM((T, HD), bf16),
-            pltpu.VMEM((NH, T), f32),
+            jax.ShapeDtypeStruct((T, NH * HD), bf16),
+            jax.ShapeDtypeStruct((T, NH * HD), bf16),
+            jax.ShapeDtypeStruct((T, HD), bf16),
+            jax.ShapeDtypeStruct((T, HD), bf16),
+            jax.ShapeDtypeStruct((NH, T), f32),
         ],
         in_specs=[any_spec] * 4 + [smem] * 2,
         out_specs=[vmem] * 5,
@@ -395,12 +408,12 @@
             V((2, 4, HD, T), bf16),
             dma((2 + 2 * NCH,)),
             dma((3,)),
-            dma(()),
+            dma((2,)),
             dma((NCH,)),
             dma((NCH,)),
             dma(()),
-            dma((4,)),
-            dma((4,)),
+            dma((2, 4)),
+            dma((2, 4)),
             dma(()),
             dma((7,)),
             dma((2,)),

time: 65.4 us -> 65.2 us (level)
  the two profiles are of different devices: /device:TPU:26 before, /device:TPU:1 now
where the time goes in v5:
time: 65.2 us; the launch traced here: 64.5 us
  Pallas kernels  63.7 us (98%)
  between operations  0.8 us (1%)
    pallas_call x1, Pallas kernels, body(): pl.pallas_call(kernel, out_shape=[jax.ShapeDtypeStruct((T, NH * HD), bf16...  61.5 us
    pallas_call x1, Pallas kernels, body(): pl.pallas_call(hand_over, out_shape=[jax.ShapeDtypeStruct(a.shape, a.dtyp...  2.27 us

profile of v5, /device:TPU:1, one launch (start us, length us, event | category | flops | bytes accessed | tf_op | source)
XLA Modules:
  0.0 64.5 jit_solution(3668911354753783025)
XLA Ops:
  0.6 61.5 %attention.1 = (bf16[256,1024]{1,0:T(8,128)(2,1)}, bf16[256,1024]{1,0:T(8,128)(2,1)}, bf16[256,128]{1,0:T(8,128)(2,1)}, bf16[256,128]{1,0:T(8,128)(2,1)}, f32[8,256]{1,0:T(8,128)}) custom-call(bf16[32,8192]{1,0:T(8,128)(2,1)} %q_in.1, bf16[32,1024]{1,0:T(8,128)(2,1)} %k_in.1, bf16[32,1024]{1,0:T(8,128)(2,1)} %v_in.1, bf16[32,8192]{1,0:T(8,128)(2,1)} %do_in.1, ...), custom_call_target="tpu_custom_call" | custom-call | flops 8000000000 | bytes 6291456 | tf_op jit(solution)/shard_map/attention/pallas_call | solution.py:380
  62.1 2.3 %hand_over.1 = (bf16[256,1024]{1,0:T(8,128)(2,1)}, bf16[256,1024]{1,0:T(8,128)(2,1)}, bf16[256,128]{1,0:T(8,128)(2,1)}, bf16[256,128]{1,0:T(8,128)(2,1)}, f32[8,256]{1,0:T(8,128)}) custom-call(bf16[256,1024]{1,0:T(8,128)(2,1)} %get-tuple-element.10.refs_0_, bf16[256,1024]{1,0:T(8,128)(2,1)} %get-tuple-element.11.refs_1_, ...), custom_call_target="tpu_custom_call" | custom-call | tf_op jit(solution)/shard_map/hand_over/pallas_call | solution.py:431
